TPU v7x, 128 devices: a whole 4x4x4 slice. The times are simulated.
128 devices in a mesh: loop: 2 (over z_lo), blk: 64 (over z_hi, x, y, core).
Axes of the slice: x: 4, y: 4, z: 4 (z_hi: 2, z_lo: 2; z = z_hi * 2 + z_lo), core: 2. Of those that a mesh axis runs over, the one named last changes fastest.
Arguments:
- queries: bfloat16 [2, 8192, 4096], P('loop', 'blk'), may hold values from -60 to 60
- keys: bfloat16 [2, 8192, 512], P('loop', 'blk'), may hold values from -60 to 60
- values: bfloat16 [2, 8192, 512], P('loop', 'blk'), may hold values from -6 to 6
- match: int32 [128], P(('loop', 'blk')), may hold values from 0 to 1
- dec_queries: bfloat16 [2, 4096, 4096], P(None, ('loop', 'blk')), may hold values from -60 to 60
- new_keys: bfloat16 [2, 4096, 512], P(None, ('loop', 'blk')), may hold values from -60 to 60
- new_values: bfloat16 [2, 4096, 512], P(None, ('loop', 'blk')), may hold values from -6 to 6
- row_len: int32 [4096], P(('loop', 'blk')), may hold values from 1024 to 8192, as said below
Outputs:
- prompt_out: bfloat16 [2, 8192, 4096], P('loop', 'blk')
- handed_cache: bfloat16 [128, 2, 8192, 512], P(('loop', 'blk'))
- dec_out: bfloat16 [2, 4096, 4096], P(None, ('loop', 'blk'))
Inputs may be any that keep to these rules, and one draw needn't show every extreme that they name: `row_len`: the first of each device's 32 requests has 8192.
All inputs are finite; a program needn't handle non-finite values.
Results may differ from a plain program's by a relative error of at most 0.009.
Values may be sent and summed in bfloat16 or wider, within the bound.
No kernel may reach another device: no remote copies, remote signals or barrier semaphores. Data moves between devices by JAX's collectives and lax.ppermute only.
A program may use at most 256 MiB of HBM per device.

v0:
```python
import math

import jax
import jax.numpy as jnp
from jax import lax
from jax.sharding import PartitionSpec as P

HD = 128


def shifted(value, axis, steps):
    count = lax.axis_size(axis)
    pairs = [(source, (source + steps) % count) for source in range(count)]
    return lax.ppermute(value, axis, pairs)


def partner(block, axis, distance):
    count = lax.axis_size(axis)
    route = []
    for low in range(count):
        high = low | 1 << distance
        if high != low and high < count:
            route += [(low, high), (high, low)]
    return lax.ppermute(block, axis, route)


def body(queries, keys, values, match, dec_queries, new_keys, new_values, row_len):
    count = lax.axis_size("blk")
    place = lax.axis_index("blk")
    side = lax.axis_index("loop")
    tok = queries.shape[1]
    width = keys.shape[2]
    heads_kv = width // HD
    group = queries.shape[2] // width
    seq_len = tok * count
    scale = 1.0 / math.sqrt(HD)
    query = queries[0].reshape(tok, heads_kv, group, HD)
    positions = jnp.arange(tok, dtype=jnp.int32)
    stacked = jnp.stack([keys[0], values[0]])
    bounds = ((0, heads_kv, 1),)

    def consume(shard, state, cache, low, high, source):
        big, total, acc = state
        part_k = shard[0].reshape(tok, high - low, HD)
        part_v = shard[1].reshape(tok, high - low, HD)
        scores = (
            jnp.einsum("tkgd,skd->kgts", query, part_k, preferred_element_type=jnp.float32) * scale
        )
        allow = (source * tok + positions)[None, :] <= (place * tok + positions)[:, None]
        scores = jnp.where(allow, scores, -1e30)
        top = jnp.maximum(big, jnp.max(scores, axis=-1))
        weights = jnp.where(allow, jnp.exp(scores - top[..., None]), 0.0)
        shrink = jnp.exp(big - top)
        total = total * shrink + jnp.sum(weights, axis=-1)
        acc = acc * shrink[..., None] + jnp.einsum(
            "kgts,skd->kgtd",
            weights.astype(jnp.bfloat16),
            part_v,
            preferred_element_type=jnp.float32,
        )
        cache = lax.dynamic_update_slice(cache, shard, (0, source * tok, low * HD))
        return ((top, total, acc), cache)

    cache = jnp.zeros((stacked.shape[0], seq_len, width), jnp.bfloat16)
    shards = []
    states = []
    low, high, way = bounds[0]
    shard = stacked
    start = (
        jnp.full((high - low, group, tok), -1e30, jnp.float32),
        jnp.zeros((high - low, group, tok), jnp.float32),
        jnp.zeros((high - low, group, tok, HD), jnp.float32),
    )
    state, cache = consume(shard, start, cache, low, high, place)
    shards.append(shard)
    states.append(state)

    def turn(index, carry):
        moving, held, filled = carry
        moved = (shifted(moving[0], "blk", 1),)
        updated = []
        for number, (low, high, way) in enumerate(bounds):
            source = (place - way * index) % count
            state, filled = consume(moved[number], held[number], filled, low, high, source)
            updated.append(state)
        return (moved, tuple(updated), filled)

    shards, states, cache = lax.fori_loop(1, count, turn, (tuple(shards), tuple(states), cache))
    merged = jnp.concatenate([state[2] / state[1][..., None] for state in states], axis=0)
    prompt_out = (
        merged.transpose(2, 0, 1, 3).reshape(tok, heads_kv * group * HD).astype(jnp.bfloat16)[None]
    )
    prompt = match[0]
    other = partner(cache, "loop", 0)
    mine = jnp.where(prompt == side, cache, other)
    handed_cache = mine[None]
    rows = dec_queries.shape[1]
    cache_k = mine[0].reshape(seq_len, heads_kv, HD)
    cache_v = mine[1].reshape(seq_len, heads_kv, HD)
    block = min(512, seq_len)
    offsets = jnp.arange(block, dtype=jnp.int32)
    outputs = []
    for step in range(dec_queries.shape[0]):
        dquery = dec_queries[step].reshape(rows, heads_kv, group, HD)

        def scan_block(index, state):
            big, total, acc = state
            key_part = lax.dynamic_slice_in_dim(cache_k, index * block, block, 0)
            value_part = lax.dynamic_slice_in_dim(cache_v, index * block, block, 0)
            scores = (
                jnp.einsum("rkgd,skd->rkgs", dquery, key_part, preferred_element_type=jnp.float32)
                * scale
            )
            allow = ((index * block + offsets)[None, :] < row_len[:, None])[:, None, None, :]
            scores = jnp.where(allow, scores, -1e30)
            top = jnp.maximum(big, jnp.max(scores, axis=-1))
            weights = jnp.where(allow, jnp.exp(scores - top[..., None]), 0.0)
            shrink = jnp.exp(big - top)
            total = total * shrink + jnp.sum(weights, axis=-1)
            acc = acc * shrink[..., None] + jnp.einsum(
                "rkgs,skd->rkgd",
                weights.astype(jnp.bfloat16),
                value_part,
                preferred_element_type=jnp.float32,
            )
            return (top, total, acc)

        start = (
            jnp.full((rows, heads_kv, group), -1e30, jnp.float32),
            jnp.zeros((rows, heads_kv, group), jnp.float32),
            jnp.zeros((rows, heads_kv, group, HD), jnp.float32),
        )
        big, total, acc = lax.fori_loop(0, seq_len // block, scan_block, start)
        fresh_k = new_keys[: step + 1].reshape(step + 1, rows, heads_kv, HD)
        fresh_v = new_values[: step + 1].reshape(step + 1, rows, heads_kv, HD)
        fresh = (
            jnp.einsum("rkgd,jrkd->rkgj", dquery, fresh_k, preferred_element_type=jnp.float32)
            * scale
        )
        top = jnp.maximum(big, jnp.max(fresh, axis=-1))
        shrink = jnp.exp(big - top)
        fresh_w = jnp.exp(fresh - top[..., None])
        total = total * shrink + jnp.sum(fresh_w, axis=-1)
        acc = acc * shrink[..., None] + jnp.einsum(
            "rkgj,jrkd->rkgd",
            fresh_w.astype(jnp.bfloat16),
            fresh_v,
            preferred_element_type=jnp.float32,
        )
        outputs.append(
            (acc / total[..., None]).reshape(rows, heads_kv * group * HD).astype(jnp.bfloat16)
        )
    dec_out = jnp.stack(outputs)
    return (prompt_out, handed_cache, dec_out)


def solution(mesh):
    in_specs = (
        P("loop", "blk", None),
        P("loop", "blk", None),
        P("loop", "blk", None),
        P(("loop", "blk")),
        P(None, ("loop", "blk"), None),
        P(None, ("loop", "blk"), None),
        P(None, ("loop", "blk"), None),
        P(("loop", "blk")),
    )
    out_specs = (
        P("loop", "blk", None),
        P(("loop", "blk"), None, None, None),
        P(None, ("loop", "blk"), None),
    )
    return jax.shard_map(body, mesh=mesh, in_specs=in_specs, out_specs=out_specs, check_vma=False)
```

profile of v0, /device:TPU:0, one launch (start us, length us, event | category | flops | bytes accessed | tf_op | source)
XLA Modules:
  0.0 1621.2 jit_solution(4303659681460121332)
XLA Ops:
  21.1 992.5 %while.61 = (s32[]{:T(128)}, bf16[2,128,512]{1,2,0:T(8,128)(2,1)}, f32[4,8,128]{2,1,0:T(8,128)S(1)}, f32[4,8,128]{2,1,0:T(8,128)S(1)}, f32[4,8,128,128]{3,2,1,0:...) while((s32[]{:T(128)}, bf16[2,128,512]{1,2,0:T(8,128)(2,1)}, ...), condition=%wide.region_5.6_spmd.clone.clone, body=%wide.region_2.5_spmd.clone.clone.sunk | while | flops 276324608 | bytes 14748008 | solution.py:88
  21.2 12.2 collective-permute-done
  37.6 11.6 collective-permute-done
  53.3 11.6 collective-permute-done
  69.1 11.6 collective-permute-done
  84.8 11.6 collective-permute-done
  100.5 11.6 collective-permute-done
  163.5 11.6 collective-permute-done
  195.0 11.6 collective-permute-done
  210.8 11.6 collective-permute-done
  226.5 11.6 collective-permute-done
  242.2 11.6 collective-permute-done
  273.7 11.6 collective-permute-done
  321.0 11.6 collective-permute-done
  336.7 11.6 collective-permute-done
  352.5 11.6 collective-permute-done
  383.9 11.6 collective-permute-done
  399.7 11.6 collective-permute-done
  1013.6 21.3 %copy.98 = bf16[2,8192,512]{2,1,0:T(8,128)(2,1)} copy(bf16[2,8192,512]{1,2,0:T(8,128)(2,1)} %get-tuple-element.549) | data formatting | bytes 33554432 | tf_op jit(solution)/shard_map/while | solution.py:88
  1044.5 342.9 %collective-permute-done.1 = bf16[2,8192,512]{2,1,0:T(8,128)(2,1)} collective-permute-done((bf16[2,8192,512]{2,1,0:T(8,128)(2,1)}, bf16[2,8192,512]{2,1,0:T(8,128)(2,1)}, u32[]{:S(2)}, u32[]{:S(2)}) %collective-permute-start.1) | collective-permute-done | bytes 16777248 | tf_op jit(solution)/shard_map/ppermute | solution.py:24
  1406.9 12.6 reshape_squeeze.18
  1427.2 12.6 reshape_squeeze.16
  1447.5 78.1 %while.62 = (s32[]{:T(128)}, f32[32,4,8]{0,2,1:T(8,128)S(1)}, f32[32,4,8]{0,2,1:T(8,128)S(1)}, f32[32,4,8,128]{3,0,2,1:T(8,128)S(1)}, s32[32]{0:T(128)}, /*index...) while((s32[]{:T(128)}, f32[32,4,8]{0,2,1:T(8,128)S(1)}, ...), condition=%wide.region_9.10_spmd.clone, body=%wide.region_6.9_spmd.clone.sunk | while | flops 275666432 | bytes 8786235 | solution.py:133
  1526.4 91.6 %while.63 = (s32[]{:T(128)}, f32[32,4,8]{0,2,1:T(8,128)S(1)}, f32[32,4,8]{0,2,1:T(8,128)S(1)}, f32[32,4,8,128]{3,0,2,1:T(8,128)}, s32[32]{0:T(128)}, /*index=5*/...) while((s32[]{:T(128)}, f32[32,4,8]{0,2,1:T(8,128)S(1)}, ...), condition=%wide.region_13.14_spmd.clone, body=%wide.region_10.13_spmd.clone.sunk | while | flops 275666432 | bytes 12980595 | solution.py:133
  (1202 shorter events, 1026.4 us)
Async XLA Ops:
  21.1 12.3 collective-permute-start
  37.5 11.7 collective-permute-start
  53.2 11.7 collective-permute-start
  69.0 11.7 collective-permute-start
  84.7 11.7 collective-permute-start
  100.4 11.7 collective-permute-start
  163.4 11.7 collective-permute-start
  194.9 11.7 collective-permute-start
  210.7 11.7 collective-permute-start
  226.4 11.7 collective-permute-start
  242.1 11.7 collective-permute-start
  273.6 11.7 collective-permute-start
  320.9 11.7 collective-permute-start
  336.6 11.7 collective-permute-start
  352.4 11.7 collective-permute-start
  383.8 11.7 collective-permute-start
  399.6 11.7 collective-permute-start
  431.1 11.7 collective-permute-start
  462.6 11.7 collective-permute-start
  494.1 11.7 collective-permute-start
  509.8 11.7 collective-permute-start
  525.6 11.7 collective-permute-start
  541.3 11.7 collective-permute-start
  1034.9 352.5 %collective-permute-start.1 = (bf16[2,8192,512]{2,1,0:T(8,128)(2,1)}, bf16[2,8192,512]{2,1,0:T(8,128)(2,1)}, u32[]{:S(2)}, u32[]{:S(2)}) collective-permute-start(bf16[2,8192,512]{2,1,0:T(8,128)(2,1)} %copy.98), channel_id=1, source_target_pairs={{0,64},{64,0},{1,65},{65,1},{2,66},{66,2},{3,67},{67,3},{4,68},{68... | collective-permute-start | bytes 50331656 | tf_op jit(solution)/shard_map/ppermute | solution.py:24
  (83 other events, 929.7 us)
where the time goes:
time: 1630 us; the launch traced here: 1620 us
  waiting for transfers between devices  1080 us (66%)
  matrix products  238 us (15%)
  local copies, waits for them, and re-layouts  199 us (12%)
  other arithmetic  99 us (6%)
    ppermute x63, waiting for transfers between devices, shifted(): return lax.ppermute(value, axis, pairs)  733 us
    ppermute x1, waiting for transfers between devices, partner(): return lax.ppermute(block, axis, route)  343 us
    dot_general x64, matrix products, consume(): jnp.einsum('kgts,skd->kgtd', weights.astype(jnp.bfloat16), part_v, prefer...  92.7 us
    dot_general x32, matrix products, scan_block(): jnp.einsum('rkgs,skd->rkgd', weights.astype(jnp.bfloat16), value_part, pr...  58.8 us
    while x222, local copies, waits for them, and re-layouts  57.2 us
    dot_general x32, matrix products, scan_block(): jnp.einsum('rkgd,skd->rkgs', dquery, key_part, preferred_element_type=jnp...  50.9 us
    dynamic_update_slice x63, local copies, waits for them, and re-layouts, consume(): cache = lax.dynamic_update_slice(cache, shard, (0, source * tok, low * HD))  45.3 us
    reduce_sum x64, other arithmetic, consume(): total = total * shrink + jnp.sum(weights, axis=-1)  35.4 us
  transfers between devices with their start and end apart: 64, of which 64 were waited for; matrix products, arithmetic and copies ran while one was open for 1% of the time, Pallas kernels for 0%

commit v1 on v0

v1 whole, which is shorter than its diff:
```python
import functools
import math

import jax
import jax.numpy as jnp
from jax import lax
from jax.experimental import pallas as pl
from jax.experimental.pallas import tpu as pltpu
from jax.sharding import PartitionSpec as P

HD = 128
TOK = 128
SEG = 48
ROWS = TOK + SEG
AX = ("loop", "blk")
ROTS = ("xyz", "yzx", "zxy")
LEAD = (0, 1, 0)
SCALE = 1.0 / math.sqrt(HD)
LOG2 = math.log2(math.e) * SCALE
NEG = -1e30
BIG = 1 << 30
LIMIT = 100.0


def index(x, y, z, c):
    return (z % 2) * 64 + (((z // 2) * 4 + x) * 4 + y) * 2 + c


def moved(value, dim, rule):
    at = "xyz".index(dim)
    route = []
    for flat in range(128):
        c, y, x, z = flat % 2, flat // 2 % 4, flat // 8 % 4, flat // 32
        there = [x, y, z]
        there[at] = rule(there[at], c) % 4
        route.append((index(x, y, z, c), index(*there, c)))
    return lax.ppermute(value, AX, route)


def swapped(value):
    return lax.ppermute(value, AX, [(i, i ^ 1) for i in range(128)])


def tied(values):
    return list(lax.optimization_barrier(tuple(values)))


def dot_nt(a, b):
    return lax.dot_general(a, b, (((1,), (1,)), ((), ())), preferred_element_type=jnp.float32)


def dot_nn(a, b):
    return lax.dot_general(a, b, (((1,), (0,)), ((), ())), preferred_element_type=jnp.float32)


def lane_sums(w):
    total = w[:, :128]
    for at in range(128, w.shape[1], 128):
        total = total + w[:, at : at + 128]
    return total


def positions(bases, n, live):
    it = lax.broadcasted_iota(jnp.int32, (1, len(bases) * n), 1)
    pos = it + bases[0]
    inside = it
    for s in range(1, len(bases)):
        pos = jnp.where(it >= s * n, it + (bases[s] - s * n), pos)
        inside = jnp.where(it >= s * n, it - s * n, inside)
    return jnp.where(inside < live, pos, BIG)


def stage_kernel(stage, meta, lens, q, dq, o0, o1, o2, s0, s1, s2, *rest):
    last = stage == 3
    accs_in, rest = rest[:4], rest[5:]
    if last:
        (pout, dout, handed, mx), rest = rest[:4], rest[4:]
        accs_out = None
    else:
        accs_out, handed, mx, rest = rest[:4], rest[4], rest[5], rest[6:]
    buf, sp, sl, dp, dl, load_sem, acc_sem, out_sem, hand_sem = rest
    accs = (sp, sl, dp, dl)
    px, py, pz, core, match = meta[0], meta[1], meta[2], meta[3], meta[4]
    mine = (((pz >> 1) * 4 + px) * 4 + py) * 2 + core
    same = match == (pz & 1)
    odd = stage % 2 == 1

    loads = [
        pltpu.make_async_copy(src, buf.at[r, side], load_sem.at[r, side])
        for r, pair in enumerate(((o0, s0), (o1, s1), (o2, s2)))
        for side, src in enumerate(pair)
    ]
    for copy in loads:
        copy.start()
    first = 2 if stage == 0 else 0
    acc_loads = [
        pltpu.make_async_copy(accs_in[i], accs[i], acc_sem.at[i]) for i in range(first, 4)
    ]
    for copy in acc_loads:
        copy.start()
    if stage == 0:
        sp[...] = jnp.zeros_like(sp)
        sl[...] = jnp.zeros_like(sl)
    for copy in acc_loads:
        copy.wait()
    for copy in loads:
        copy.wait()

    def place(r, side, lead, inner):
        cs = core if side == 0 else 1 - core

        def offset(i):
            return jnp.where(
                i == 0, 0, jnp.where(i == 3, 2, jnp.where(i == 1, 1 + 2 * cs, 3 - 2 * cs))
            )

        turn = stage * (2 * cs - 1)
        el, ei = offset(lead), offset(inner)
        x = jnp.where(r == 0, px ^ el, jnp.where(r == 1, (px + turn) & 3, px ^ ei))
        y = jnp.where(r == 2, (py + turn) & 3, py ^ ei)
        z = jnp.where(r == 0, (pz + turn) & 3, pz ^ el)
        return (((z >> 1) * 4 + x) * 4 + y) * 2 + cs

    def facing(lead):
        return jnp.where(lead == 1, 2, jnp.where(lead == 2, 1, lead))

    def lead_of(item, own):
        r = jnp.where(item < 2, 1, jnp.where(item < 4, 2, 0))
        near = jnp.where(item % 2 == 0, 0, 3)
        far = 1 + item % 2
        lead = jnp.where(item >= 4, item - 4, jnp.where(own, near, far))
        return r, lead

    def hand(r, lead, act):
        live = min(SEG, TOK - SEG * r)
        for side in range(2):
            at = lead if side == 0 else facing(lead)
            for inner in range(4):
                row = place(r, side, at, inner) * TOK
                for half in range(2):
                    lanes = pl.ds(half * HD, HD)
                    for lo, n, to, head in ((0, TOK, 0, r), (TOK, live, SEG * r, 3)):
                        act(
                            pltpu.make_async_copy(
                                buf.at[r, side, at, inner, pl.ds(lo, n), lanes],
                                handed.at[
                                    half,
                                    pl.ds(pl.multiple_of(row + to, 16), n),
                                    pl.ds(head * HD, HD),
                                ],
                                hand_sem,
                            )
                        )

    def hand_all(act):
        for r in (1, 2):

            def some(i, _):
                hand(r, jnp.where(same, i * 3, 1 + i), act)
                return 0

            lax.fori_loop(0, 2, some, 0)

        @pl.when(jnp.logical_xor(same, odd))
        def _():
            def some(i, _):
                hand(0, i, act)
                return 0

            lax.fori_loop(0, 4, some, 0)

    hand_all(lambda copy: copy.start())

    high = buf[2, 0, :, :, TOK + 32 : TOK + 48, :].reshape(16, 16, 256)
    other = buf[2, 1, :, :, TOK + 32 : TOK + 48, :].reshape(16, 16, 256)
    mx[...] = jnp.max(jnp.maximum(high, other).astype(jnp.float32), axis=0)

    def main_tile(item, own):
        r, lead = lead_of(item, own)
        keys, bases = [], []
        for side in range(2):
            at = lead if side == 0 else facing(lead)
            keys.append(buf[r, side, at, :, 0:TOK, :].reshape(4 * TOK, 256))
            bases += [place(r, side, at, inner) * TOK for inner in range(4)]
        return r, jnp.concatenate(keys, 0), bases, positions(bases, TOK, TOK)

    def third_tile(item, own):
        r = jnp.where(item == 0, 1, jnp.where(item == 1, 2, 0))
        keys, bases = [], []
        for part in range(2):
            lead = jnp.where(
                item >= 2, (item - 2) * 2 + part, jnp.where(own, 3 * part, 1 + part)
            )
            for side in range(2):
                at = lead if side == 0 else facing(lead)
                keys.append(buf[r, side, at, :, TOK:ROWS, :].reshape(4 * SEG, 256))
                bases += [
                    place(r, side, at, inner) * TOK + r * SEG for inner in range(4)
                ]
        live = jnp.where(r == 2, TOK - 2 * SEG, SEG)
        return 3, jnp.concatenate(keys, 0), bases, positions(bases, SEG, live)

    def lowest(bases):
        return functools.reduce(jnp.minimum, bases)

    def prompt_tile(tile, item):
        head, kv, bases, pos = tile(item, True)

        @pl.when(lowest(bases) < mine * TOK)
        def _():
            bias = jnp.where(pos < mine * TOK, 0.0, NEG)
            k, v = kv[:, :HD], kv[:, HD:]
            for chunk in range(4):
                rows = slice(chunk * 256, chunk * 256 + 256)
                parts = []
                for g in range(2 * chunk, 2 * chunk + 2):
                    lane = pl.multiple_of((head * 8 + g) * HD, HD)
                    parts.append(q[:, pl.ds(lane, HD)])
                w = jnp.exp2(dot_nt(jnp.concatenate(parts, 0), k) * LOG2 + bias)
                sl[head, rows, :] += lane_sums(w)
                sp[head, rows, :] += dot_nn(w.astype(jnp.bfloat16), v)

    def decode_tile(tile, item):
        head, kv, bases, pos = tile(item, same)
        k, v = kv[:, :HD], kv[:, HD:]
        for chunk in range(2):
            rows = slice(chunk * 256, chunk * 256 + 256)
            parts = []
            for g in range(4 * chunk, 4 * chunk + 4):
                lane = pl.multiple_of((head * 8 + g) * HD, HD)
                parts.append(dq[:, pl.ds(lane, HD)])
            limit = jnp.concatenate([lens[:, 0:1]] * 4, 0)
            s = dot_nt(jnp.concatenate(parts, 0), k) * LOG2
            w = jnp.exp2(jnp.where(pos < limit, s, NEG))
            dl[head, rows, :] += lane_sums(w)
            dp[head, rows, :] += dot_nn(w.astype(jnp.bfloat16), v)

    if stage == 0:
        row = lax.broadcasted_iota(jnp.int32, (256, TOK), 0) % TOK
        col = lax.broadcasted_iota(jnp.int32, (256, TOK), 1)
        for head in range(4):
            if head < 3:
                kv = buf[head, 0, 0, 0, 0:TOK, :]
            else:
                kv = jnp.concatenate(
                    [
                        buf[r, 0, 0, 0, TOK : TOK + min(SEG, TOK - SEG * r), :]
                        for r in range(3)
                    ],
                    0,
                )
            k, v = kv[:, :HD], kv[:, HD:]
            for chunk in range(4):
                rows = slice(chunk * 256, chunk * 256 + 256)
                parts = [
                    q[:, (head * 8 + g) * HD : (head * 8 + g + 1) * HD]
                    for g in (2 * chunk, 2 * chunk + 1)
                ]
                s = dot_nt(jnp.concatenate(parts, 0), k) * LOG2
                w = jnp.exp2(jnp.where(col <= row, s, NEG))
                sl[head, rows, :] += lane_sums(w)
                sp[head, rows, :] += dot_nn(w.astype(jnp.bfloat16), v)

    def loop(count, work, tile):
        def one(i, _):
            work(tile, i)
            return 0

        lax.fori_loop(0, count, one, 0)

    spread = jnp.where(jnp.logical_xor(same, odd), 1, 0)
    loop(4 if odd else 8, prompt_tile, main_tile)
    loop(2 if odd else 4, prompt_tile, third_tile)
    loop(4 + 4 * spread, decode_tile, main_tile)
    loop(2 + 2 * spread, decode_tile, third_tile)

    if last:
        for head in range(4):
            for g in range(8):
                lanes = slice((head * 8 + g) * HD, (head * 8 + g + 1) * HD)
                rows = slice(g * TOK, (g + 1) * TOK)
                total = jnp.sum(sl[head, rows, :], axis=1, keepdims=True)
                pout[:, lanes] = (sp[head, rows, :] / total).astype(jnp.bfloat16)
                rows = slice(g * 64, (g + 1) * 64)
                total = jnp.sum(dl[head, rows, :], axis=1, keepdims=True)
                dout[:, lanes] = (dp[head, rows, :] / total).astype(jnp.bfloat16)
    else:
        stores = [
            pltpu.make_async_copy(accs[i], accs_out[i], out_sem.at[i]) for i in range(4)
        ]
        for copy in stores:
            copy.start()
        for copy in stores:
            copy.wait()
    hand_all(lambda copy: copy.wait())


def run_stage(stage, meta, lens, q, dq, own, sib, accs, handed):
    anywhere = pl.BlockSpec(memory_space=pl.ANY)
    vmem = pl.BlockSpec(memory_space=pltpu.VMEM)
    acc_shapes = [jax.ShapeDtypeStruct(a.shape, a.dtype) for a in accs]
    handed_shape = jax.ShapeDtypeStruct((2, 8192, 512), jnp.bfloat16)
    mx_shape = jax.ShapeDtypeStruct((16, 256), jnp.float32)
    if stage == 3:
        outs = [
            jax.ShapeDtypeStruct(q.shape, jnp.bfloat16),
            jax.ShapeDtypeStruct(dq.shape, jnp.bfloat16),
            handed_shape,
            mx_shape,
        ]
        specs = [vmem, vmem, anywhere, vmem]
        alias = {14: 2}
    else:
        outs = [*acc_shapes, handed_shape, mx_shape]
        specs = [anywhere] * 5 + [vmem]
        alias = {10: 0, 11: 1, 12: 2, 13: 3, 14: 4}
    units = (2 * 64 if stage % 2 == 0 else 2 * 32) * 128
    return pl.pallas_call(
        functools.partial(stage_kernel, stage),
        out_shape=outs,
        in_specs=[pl.BlockSpec(memory_space=pltpu.SMEM), vmem, vmem, vmem] + [anywhere] * 11,
        out_specs=specs,
        input_output_aliases=alias,
        scratch_shapes=[
            pltpu.VMEM((3, 2, 4, 4, ROWS, 256), jnp.bfloat16),
            pltpu.VMEM((4, 1024, HD), jnp.float32),
            pltpu.VMEM((4, 1024, HD), jnp.float32),
            pltpu.VMEM((4, 512, HD), jnp.float32),
            pltpu.VMEM((4, 512, HD), jnp.float32),
            pltpu.SemaphoreType.DMA((3, 2)),
            pltpu.SemaphoreType.DMA((4,)),
            pltpu.SemaphoreType.DMA((4,)),
            pltpu.SemaphoreType.DMA,
        ],
        compiler_params=pltpu.CompilerParams(vmem_limit_bytes=40 * 2**20),
        cost_estimate=pl.CostEstimate(
            flops=units * 1024 * 512, bytes_accessed=30 << 20, transcendentals=units * 1024
        ),
        name=f"stage{stage}",
    )(meta, lens, q, dq, *own, *sib, *accs, handed)


def fresh_part(dec_queries, new_keys, new_values):
    steps, rows = dec_queries.shape[:2]
    dq = dec_queries.reshape(steps, rows, 4, 8, HD).astype(jnp.float32)
    nk = new_keys.reshape(steps, rows, 4, 1, HD).astype(jnp.float32)
    nv = new_values.reshape(steps, rows, 4, 1, HD).astype(jnp.float32)
    acc = total = 0.0
    for j in range(steps):
        s = jnp.sum(dq * nk[j], axis=-1, keepdims=True) * LOG2
        allow = (jnp.arange(steps) >= j).reshape(steps, 1, 1, 1, 1)
        w = jnp.exp2(jnp.where(allow, s, NEG))
        total = total + w
        acc = acc + w.astype(jnp.bfloat16).astype(jnp.float32) * nv[j]
    total = jnp.broadcast_to(total / HD, acc.shape)

    def rowwise(v):
        return v.transpose(2, 3, 0, 1, 4).reshape(4, 8 * steps * rows, HD)

    return rowwise(acc), rowwise(total)


def careful(queries, keys, values, handed, dec_queries, new_keys, new_values, row_len):
    place = lax.axis_index("blk")
    tok, block = TOK, 512
    all_k = lax.all_gather(keys[0], "blk", tiled=True).reshape(-1, 4, HD)
    all_v = lax.all_gather(values[0], "blk", tiled=True).reshape(-1, 4, HD)
    seq = all_k.shape[0]

    def attend(query, cache_k, cache_v, limit, state):
        def turn(i, state):
            big, total, acc = state
            part_k = lax.dynamic_slice_in_dim(cache_k, i * block, block, 0)
            part_v = lax.dynamic_slice_in_dim(cache_v, i * block, block, 0)
            s = jnp.einsum("tkgd,skd->kgts", query, part_k, preferred_element_type=jnp.float32)
            s = s * SCALE
            allow = (i * block + jnp.arange(block))[None, :] < limit[:, None]
            s = jnp.where(allow, s, NEG)
            top = jnp.maximum(big, jnp.max(s, axis=-1))
            w = jnp.where(allow, jnp.exp(s - top[..., None]), 0.0)
            shrink = jnp.exp(big - top)
            total = total * shrink + jnp.sum(w, axis=-1)
            acc = acc * shrink[..., None] + jnp.einsum(
                "kgts,skd->kgtd",
                w.astype(jnp.bfloat16),
                part_v,
                preferred_element_type=jnp.float32,
            )
            return top, total, acc

        return lax.fori_loop(0, seq // block, turn, state)

    def finish(state, rows):
        out = state[2] / state[1][..., None]
        return out.transpose(2, 0, 1, 3).reshape(rows, 4096).astype(jnp.bfloat16)

    state = (
        jnp.full((4, 8, tok), NEG, jnp.float32),
        jnp.zeros((4, 8, tok), jnp.float32),
        jnp.zeros((4, 8, tok, HD), jnp.float32),
    )
    limit = place * tok + jnp.arange(tok) + 1
    state = attend(queries[0].reshape(tok, 4, 8, HD), all_k, all_v, limit, state)
    prompt_out = finish(state, tok)

    steps, rows = dec_queries.shape[:2]
    cache_k = handed[0].reshape(seq, 4, HD)
    cache_v = handed[1].reshape(seq, 4, HD)
    outs = []
    for step in range(steps):
        dquery = dec_queries[step].reshape(rows, 4, 8, HD)
        nk = new_keys[: step + 1].reshape(step + 1, rows, 4, HD)
        nv = new_values[: step + 1].reshape(step + 1, rows, 4, HD)
        s = jnp.einsum("rkgd,jrkd->kgrj", dquery, nk, preferred_element_type=jnp.float32) * SCALE
        top = jnp.max(s, axis=-1)
        w = jnp.exp(s - top[..., None])
        acc = jnp.einsum(
            "kgrj,jrkd->kgrd", w.astype(jnp.bfloat16), nv, preferred_element_type=jnp.float32
        )
        state = attend(dquery, cache_k, cache_v, row_len, (top, jnp.sum(w, axis=-1), acc))
        outs.append(finish(state, rows))
    return prompt_out, jnp.stack(outs)


def longest(value):
    parts = value.astype(jnp.float32).reshape(-1, HD)
    return jnp.sqrt(jnp.max(jnp.sum(parts * parts, axis=-1)))


def body(queries, keys, values, match, dec_queries, new_keys, new_values, row_len):
    flat = lax.axis_index("loop") * 64 + lax.axis_index("blk")
    core, y, x = flat % 2, flat // 2 % 4, flat // 8 % 4
    z = flat // 32 % 2 * 2 + flat // 64
    meta = jnp.stack([x, y, z, core, match[0], 0, 0, 0]).astype(jnp.int32)

    high_k = jnp.maximum(longest(keys), longest(new_keys)) * 1.01
    high_q = jnp.maximum(longest(queries), longest(dec_queries)) * 1.01
    spare = jnp.concatenate(
        [jnp.full((16, HD), high_k), jnp.full((16, HD), high_q)], axis=1
    ).astype(jnp.bfloat16)
    k, v = keys[0], values[0]

    def packed(lo, hi, head):
        lanes = slice(head * HD, (head + 1) * HD)
        return jnp.concatenate([k[lo:hi, lanes], v[lo:hi, lanes]], axis=1)

    pieces = []
    for r in range(3):
        rows = [packed(0, TOK, r), packed(SEG * r, min(SEG * (r + 1), TOK), 3)]
        if r == 2:
            rows.append(spare)
        pieces.append(jnp.concatenate(rows, 0)[None, None])

    pieces = tied(pieces)
    for phase in range(2):
        for step in range(2):
            got = tied(
                [
                    moved(p, rot[phase], lambda a, c: a ^ (1 if step == c else 3))
                    for p, rot in zip(pieces, ROTS)
                ]
            )
            axes = [lead if phase == 0 else 1 - lead for lead in LEAD]
            pieces = tied(
                [jnp.concatenate([p, g], a) for p, g, a in zip(pieces, got, axes)]
            )

    lens = jnp.broadcast_to(jnp.tile(row_len, 2)[:, None], (64, HD)).astype(jnp.int32)
    q, dq = queries[0], dec_queries.reshape(64, 4096)
    dacc, dtotal = fresh_part(dec_queries, new_keys, new_values)
    nothing = jnp.zeros((4, 1024, HD), jnp.float32)
    accs = [nothing, nothing, dacc, dtotal]
    handed = jnp.zeros((2, 8192, 512), jnp.bfloat16)
    high = []
    for stage in range(4):
        sib = [swapped(p) for p in pieces]
        if stage < 3:
            onward = [
                moved(p, rot[2], lambda a, c: a + 1 - 2 * c) for p, rot in zip(pieces, ROTS)
            ]
        res = run_stage(stage, meta, lens, q, dq, pieces, sib, accs, handed)
        if stage < 3:
            accs, handed, mx = res[:4], res[4], res[5]
            pieces = onward
        else:
            prompt_out, dec_out, handed, mx = res
        high.append(mx)
    high = functools.reduce(jnp.maximum, high)
    bound = jnp.max(high[:, :HD]) * jnp.max(high[:, HD:]) * LOG2
    prompt_out, dec_out = lax.cond(
        bound < LIMIT,
        lambda: (prompt_out, dec_out.reshape(dec_queries.shape)),
        lambda: careful(
            queries, keys, values, handed, dec_queries, new_keys, new_values, row_len
        ),
    )
    return prompt_out[None], handed[None], dec_out


def solution(mesh):
    in_specs = (
        P("loop", "blk", None),
        P("loop", "blk", None),
        P("loop", "blk", None),
        P(("loop", "blk")),
        P(None, ("loop", "blk"), None),
        P(None, ("loop", "blk"), None),
        P(None, ("loop", "blk"), None),
        P(("loop", "blk")),
    )
    out_specs = (
        P("loop", "blk", None),
        P(("loop", "blk"), None, None, None),
        P(None, ("loop", "blk"), None),
    )
    return jax.shard_map(body, mesh=mesh, in_specs=in_specs, out_specs=out_specs, check_vma=False)
```

time: 1630 us -> 761 us (0.47)
  waiting for transfers between devices: 1080 us -> 122 us
  local copies, waits for them, and re-layouts: 199 us -> 128 us
  Pallas kernels: 0 us -> 57.8 us
  matrix products: 238 us -> 272 us
  starting transfers between devices: 1.59 us -> 27.4 us
  between operations: 1.63 us -> 19.6 us
  other arithmetic: 99 us -> 116 us
    ppermute x64 -> x33, waiting for transfers between devices: 1080 us -> 74.2 us  [the longest x21 74.2 us: moved(): return lax.ppermute(value, AX, route)]
    pallas_call x0 -> x4, Pallas kernels: none -> 57.8 us  [run_stage(): pl.pallas_call(functools.partial(stage_kernel, stage), out_shape=outs, in...]
    all_gather x0 -> x2, waiting for transfers between devices: none -> 47.4 us  [the longest x1 47.4 us: careful(): all_v = lax.all_gather(values[0], 'blk', tiled=True).reshape(-1, 4, HD)]
    dynamic_update_slice x63 -> x0, local copies, waits for them, and re-layouts: 45.3 us -> none  [consume(): cache = lax.dynamic_update_slice(cache, shard, (0, source * tok, low * HD))]
    reduce_sum x97 -> x54, other arithmetic: 56.5 us -> 98.1 us  [the longest x48 95.8 us: turn(): total = total * shrink + jnp.sum(w, axis=-1)]
    dot_general x195 -> x99, matrix products: 238 us -> 272 us  [the longest x48 145 us: turn(): jnp.einsum('tkgd,skd->kgts', query, part_k, preferred_element_type=jnp.fl...]
    ppermute x64 -> x33, starting transfers between devices: 1.59 us -> 27.3 us  [the longest x21 23.3 us: moved(): return lax.ppermute(value, AX, route)]
    unnamed x31 -> x59, local copies, waits for them, and re-layouts: 33.2 us -> 10.5 us
  transfers between devices with their start and end apart: 64 -> 35, of which waited for: 64 -> 18; matrix products, arithmetic and copies ran while one was open for 1% -> 28% of each run, Pallas kernels for 0% -> 6%
where the time goes in v1:
time: 761 us; the launch traced here: 746 us
  matrix products  272 us (36%)
  local copies, waits for them, and re-layouts  128 us (17%)
  waiting for transfers between devices  122 us (16%)
  other arithmetic  116 us (15%)
  Pallas kernels  57.8 us (8%)
  starting transfers between devices  27.4 us (4%)
  between operations  19.6 us (3%)
    dot_general x48, matrix products, turn(): jnp.einsum('tkgd,skd->kgts', query, part_k, preferred_element_type=jnp.fl...  145 us
    dot_general x48, matrix products, turn(): jnp.einsum('kgts,skd->kgtd', w.astype(jnp.bfloat16), part_v, preferred_el...  126 us
    reduce_sum x48, other arithmetic, turn(): total = total * shrink + jnp.sum(w, axis=-1)  95.8 us
    ppermute x21, waiting for transfers between devices, moved(): return lax.ppermute(value, AX, route)  74.2 us
    pallas_call x4, Pallas kernels, run_stage(): pl.pallas_call(functools.partial(stage_kernel, stage), out_shape=outs, in...  57.8 us
    all_gather x1, waiting for transfers between devices, careful(): all_v = lax.all_gather(values[0], 'blk', tiled=True).reshape(-1, 4, HD)  47.4 us
    while x144, local copies, waits for them, and re-layouts  39 us
    while x7, local copies, waits for them, and re-layouts, attend(): return lax.fori_loop(0, seq // block, turn, state)  24.4 us
  transfers between devices with their start and end apart: 35, of which 18 were waited for; matrix products, arithmetic and copies ran while one was open for 28% of the time, Pallas kernels for 6%

profile of v1, /device:TPU:0, one launch (start us, length us, event | category | flops | bytes accessed | tf_op | source)
XLA Modules:
  0.0 745.9 jit_solution(8715835402444758445)
XLA Ops:
  45.1 6.2 collective-permute-done.6
  58.0 8.0 %collective-permute-done.10 = bf16[2,4,176,256]{3,2,1,0:T(8,128)(2,1)S(1)} collective-permute-done((bf16[2,4,176,256]{3,2,1,0:T(8,128)(2,1)S(1)}, bf16[2,4,176,256]{3,2,1,0:T(8,128)(2,1)S(1)}, u32[]{:S(2)}, u32[]{:S(2)}) %collective-permute-start.10) | collective-permute-done | bytes 720928 | tf_op jit(solution)/shard_map/ppermute | solution.py:37
  77.3 13.9 %collective-permute-done.15.o0 = bf16[4,4,176,256]{3,2,1,0:T(8,128)(2,1)S(1)} collective-permute-done((bf16[4,4,176,256]{3,2,1,0:T(8,128)(2,1)S(1)}, bf16[4,4,176,256]{3,2,1,0:T(8,128)(2,1)S(1)}, u32[]{:S(2)}, u32[]{:S(2)}) %collective-permute-start.15) | collective-permute-done | bytes 1441824 | tf_op jit(solution)/shard_map/ppermute | solution.py:37
  99.7 13.0 %collective-permute-done.21.o0 = bf16[4,4,176,256]{3,2,1,0:T(8,128)(2,1)} collective-permute-done((bf16[4,4,176,256]{3,2,1,0:T(8,128)(2,1)S(1)}, bf16[4,4,176,256]{3,2,1,0:T(8,128)(2,1)}, u32[]{:S(2)}, u32[]{:S(2)}) %collective-permute-start.21) | collective-permute-done | bytes 1441824 | tf_op jit(solution)/shard_map/ppermute | solution.py:37
  122.1 12.3 %collective-permute-done.27.o0 = bf16[4,4,176,256]{3,2,1,0:T(8,128)(2,1)} collective-permute-done((bf16[4,4,176,256]{3,2,1,0:T(8,128)(2,1)}, bf16[4,4,176,256]{3,2,1,0:T(8,128)(2,1)}, u32[]{:S(2)}, u32[]{:S(2)}) %collective-permute-start.27) | collective-permute-done | bytes 1441824 | tf_op jit(solution)/shard_map/ppermute | solution.py:37
  139.2 6.9 broadcast_in_dim.178.rest_4_
  148.9 16.1 %stage0.1 = (f32[4,1024,128]{2,1,0:T(8,128)S(1)}, f32[4,1024,128]{2,1,0:T(8,128)}, f32[4,512,128]{2,1,0:T(8,128)S(1)}, f32[4,512,128]{2,1,0:T(8,128)S(1)}, bf16[...) custom-call(s32[8]{0:T(128)S(1)} %stack.24.meta, ...), custom_call_target="tpu_custom_call", output_to_operand_aliasing={{0}: (10, {}), {1}: (11, {}), {2}: (12, {}), {3}: (13, {}),... | custom-call | flops 8589934592 | bytes 31457280 | tf_op jit(solution)/shard_map/stage0/pallas_call | solution.py:318
  165.1 11.7 %stage1.1 = (f32[4,1024,128]{2,1,0:T(8,128)S(1)}, f32[4,1024,128]{2,1,0:T(8,128)}, f32[4,512,128]{2,1,0:T(8,128)S(1)}, f32[4,512,128]{2,1,0:T(8,128)S(1)}, bf16[...) custom-call(s32[8]{0:T(128)S(1)} %stack.24.meta, ...), custom_call_target="tpu_custom_call", output_to_operand_aliasing={{0}: (10, {}), {1}: (11, {}), {2}: (12, {}), {3}: (13, {}),... | custom-call | flops 4294967296 | bytes 31457280 | tf_op jit(solution)/shard_map/stage1/pallas_call | solution.py:318
  176.8 17.4 %stage2.1 = (f32[4,1024,128]{2,1,0:T(8,128)S(1)}, f32[4,1024,128]{2,1,0:T(8,128)}, f32[4,512,128]{2,1,0:T(8,128)S(1)}, f32[4,512,128]{2,1,0:T(8,128)S(1)}, bf16[...) custom-call(s32[8]{0:T(128)S(1)} %stack.24.meta, ...), custom_call_target="tpu_custom_call", output_to_operand_aliasing={{0}: (10, {}), {1}: (11, {}), {2}: (12, {}), {3}: (13, {}),... | custom-call | flops 8589934592 | bytes 31457280 | tf_op jit(solution)/shard_map/stage2/pallas_call | solution.py:318
  194.3 12.6 %stage3.1 = (bf16[128,4096]{1,0:T(8,128)(2,1)}, bf16[64,4096]{1,0:T(8,128)(2,1)}, bf16[2,8192,512]{2,1,0:T(8,128)(2,1)}, f32[16,256]{1,0:T(8,128)S(1)}) custom-call(s32[8]{0:T(128)S(1)} %stack.24.meta, s32[64,128]{1,0:T(8,128)S(1)} %broadcast_in_dim.169.lens, bf16[128,4096]{1,0:T(8,128)(2,1)S(1)} %bitcast.232, ...), custom_call_target="tpu_custom_call", output_to_operand_aliasing={{2}: (14, {})} | custom-call | flops 4294967296 | bytes 31457280 | tf_op jit(solution)/shard_map/stage3/pallas_call | solution.py:318
  208.8 530.0 %conditional.1 = (bf16[2,32,4096]{2,1,0:T(8,128)(2,1)}, bf16[1,128,4096]{2,1,0:T(8,128)(2,1)}) conditional(s32[]{:T(128)} %convert_element_type.161, (bf16[2,32,512]{2,1,0:T(8,128)(2,1)S(1)}, bf16[2,32,4096]{2,1,0:T(8,128)(2,1)S(1)}, bf16[2,32,512]{2,1,0:T(8,128)(2,1)S(1)}, bf16[2,8192,512]{2,1,0:T(8,128)(2,1)}, s32[32]{0:T(128)S(1)}, ...), branch_computations={%region_12.27_spmd, %region_27.28_spmd} | conditional | flops 1657037568 | bytes 275319104 | solution.py:490
  212.6 21.4 %copy.147 = bf16[2,8192,512]{1,2,0:T(8,128)(2,1)} copy(bf16[2,8192,512]{2,1,0:T(8,128)(2,1)} %get-tuple-element.717) | data formatting | bytes 33554432 | tf_op jit(solution)/shard_map
  233.9 11.6 %fusion.80 = (bf16[1,8192,512]{1,2,0:T(8,128)(2,1)}, bf16[1,8192,512]{1,2,0:T(8,128)(2,1)}) fusion(bf16[2,8192,512]{1,2,0:T(8,128)(2,1)} %copy.147), kind=kLoop, calls=%fused_computation.143 | loop fusion | bytes 33554432 | tf_op jit(solution)/shard_map/cond/branch_0_fun/slice | solution.py:408
  245.5 11.9 %copy.122 = bf16[8192,4,128]{2,0,1:T(8,128)(2,1)} copy(bf16[8192,4,128]{0,2,1:T(8,128)(2,1)} %bitcast.234) | data formatting | bytes 16777216 | tf_op jit(solution)/shard_map/cond/branch_0_fun/while | solution.py:391
  257.5 12.0 %copy.124 = bf16[8192,4,128]{2,0,1:T(8,128)(2,1)} copy(bf16[8192,4,128]{0,2,1:T(8,128)(2,1)} %bitcast.233) | data formatting | bytes 16777216 | tf_op jit(solution)/shard_map/cond/branch_0_fun/while | solution.py:391
  269.5 68.8 %while.50 = (s32[]{:T(128)}, f32[4,8,32]{2,1,0:T(8,128)S(1)}, f32[4,8,32]{2,1,0:T(8,128)S(1)}, f32[4,8,32,128]{3,2,1,0:T(8,128)S(1)}, s32[32]{0:T(128)S(1)}, /*i...) while((s32[]{:T(128)}, f32[4,8,32]{2,1,0:T(8,128)S(1)}, ...), condition=%wide.region_22.22_spmd, body=%wide.region_19.21_spmd.sunk | while | flops 275532288 | bytes 8786223 | solution.py:391
  338.9 68.7 %while.49 = (s32[]{:T(128)}, f32[4,8,32]{2,1,0:T(8,128)S(1)}, f32[4,8,32]{2,1,0:T(8,128)S(1)}, f32[4,8,32,128]{3,2,1,0:T(8,128)S(1)}, s32[32]{0:T(128)S(1)}, /*i...) while((s32[]{:T(128)}, f32[4,8,32]{2,1,0:T(8,128)S(1)}, ...), condition=%wide.region_16.16_spmd, body=%wide.region_13.15_spmd.sunk | while | flops 275532288 | bytes 8786223 | solution.py:391
  410.3 47.4 %all-gather.7.cloned.1.call-done = bf16[1,8192,512]{1,2,0:T(8,128)(2,1)} async-done(((bf16[1,128,512]{1,2,0:T(8,128)(2,1)}), bf16[1,8192,512]{1,2,0:T(8,128)(2,1)}) %all-gather.7.cloned.1.call-update) | async-done | bytes 8388624 | tf_op jit(solution)/shard_map/cond/branch_0_fun/all_gather | solution.py:367
  457.7 277.3 %while.51 = (s32[]{:T(128)}, f32[4,8,128]{2,1,0:T(8,128)S(1)}, f32[4,8,128]{2,1,0:T(8,128)S(1)}, f32[4,8,128,128]{3,2,1,0:T(8,128)}, bf16[8192,4,128]{0,2,1:T(8,...) while((s32[]{:T(128)}, f32[4,8,128]{2,1,0:T(8,128)S(1)}, ...), condition=%wide.region_26.26_spmd.clone, body=%wide.region_23.25_spmd.clone.sunk | while | flops 1102664448 | bytes 82318608 | solution.py:391
  457.8 5.9 fusion.121
  475.2 5.9 fusion.121
  492.5 5.9 fusion.121
  579.1 5.9 fusion.121
  665.8 5.9 fusion.121
  (724 shorter events, 471.0 us)
Async XLA Ops:
  31.8 8.4 %collective-permute-start.3 = (bf16[2,1,176,256]{3,2,1,0:T(8,128)(2,1)S(1)}, bf16[2,1,176,256]{3,2,1,0:T(8,128)(2,1)S(1)}, u32[]{:S(2)}, u32[]{:S(2)}) collective-permute-start(bf16[2,1,176,256]{3,2,1,0:T(8,128)(2,1)S(1)} %pad_maximum_fusion.10), channel_id=1, source_target_pairs={{0,24},{1,9},{2,26},{3,11},{4,28},{5,13},{6,30},{7,15},{8,16},{9,1... | collective-permute-start | bytes 540680 | tf_op jit(solution)/shard_map/ppermute | solution.py:37
  52.2 13.8 %collective-permute-start.10 = (bf16[2,4,176,256]{3,2,1,0:T(8,128)(2,1)S(1)}, bf16[2,4,176,256]{3,2,1,0:T(8,128)(2,1)S(1)}, u32[]{:S(2)}, u32[]{:S(2)}) collective-permute-start(bf16[2,4,176,256]{3,2,1,0:T(8,128)(2,1)S(1)} %pad_maximum_fusion.5), channel_id=1, source_target_pairs={{0,96},{1,65},{2,98},{3,67},{4,100},{5,69},{6,102},{7,71},{8,104},... | collective-permute-start | bytes 2162696 | tf_op jit(solution)/shard_map/ppermute | solution.py:37
  56.7 12.5 %collective-permute-start.11 = (bf16[4,2,176,256]{3,2,1,0:T(8,128)(2,1)S(1)}, bf16[4,2,176,256]{3,2,1,0:T(8,128)(2,1)S(1)}, u32[]{:S(2)}, u32[]{:S(2)}) collective-permute-start(bf16[4,2,176,256]{3,2,1,0:T(8,128)(2,1)S(1)} %pad_maximum_fusion.6), channel_id=1, source_target_pairs={{0,24},{1,9},{2,26},{3,11},{4,28},{5,13},{6,30},{7,15},{8,16},{9,1... | collective-permute-start | bytes 2162696 | tf_op jit(solution)/shard_map/ppermute | solution.py:37
  58.0 12.5 %collective-permute-start.9 = (bf16[4,2,176,256]{3,2,1,0:T(8,128)(2,1)S(1)}, bf16[4,2,176,256]{3,2,1,0:T(8,128)(2,1)S(1)}, u32[]{:S(2)}, u32[]{:S(2)}) collective-permute-start(bf16[4,2,176,256]{3,2,1,0:T(8,128)(2,1)S(1)} %pad_maximum_fusion.4), channel_id=1, source_target_pairs={{0,6},{1,3},{2,4},{3,1},{4,2},{5,7},{6,0},{7,5},{8,14},{9,11},{10,... | collective-permute-start | bytes 2162696 | tf_op jit(solution)/shard_map/ppermute | solution.py:37
  71.0 20.3 %collective-permute-start.15 = (bf16[4,4,176,256]{3,2,1,0:T(8,128)(2,1)S(1)}, bf16[4,4,176,256]{3,2,1,0:T(8,128)(2,1)S(1)}, u32[]{:S(2)}, u32[]{:S(2)}) collective-permute-start(bf16[4,4,176,256]{3,2,1,0:T(8,128)(2,1)S(1)} %pad_maximum_fusion.1.o0), channel_id=1, source_target_pairs={{0,64},{1,97},{2,66},{3,99},{4,68},{5,101},{6,70},{7,103},{8,72},{... | collective-permute-start | bytes 4325384 | tf_op jit(solution)/shard_map/ppermute | solution.py:37
  73.9 17.4 %collective-permute-start.13 = (bf16[4,4,176,256]{3,2,1,0:T(8,128)(2,1)S(1)}, bf16[4,4,176,256]{3,2,1,0:T(8,128)(2,1)S(1)}, u32[]{:S(2)}, u32[]{:S(2)}) collective-permute-start(bf16[4,4,176,256]{3,2,1,0:T(8,128)(2,1)S(1)} %pad_maximum_fusion.2.o1), channel_id=1, source_target_pairs={{0,1},{1,0},{2,3},{3,2},{4,5},{5,4},{6,7},{7,6},{8,9},{9,8},{10,11... | collective-permute-start | bytes 4325384 | tf_op jit(solution)/shard_map/ppermute | solution.py:41
  73.9 20.3 %collective-permute-start.16 = (bf16[4,4,176,256]{3,2,1,0:T(8,128)(2,1)S(1)}, bf16[4,4,176,256]{3,2,1,0:T(8,128)(2,1)S(1)}, u32[]{:S(2)}, u32[]{:S(2)}) collective-permute-start(bf16[4,4,176,256]{3,2,1,0:T(8,128)(2,1)S(1)} %pad_maximum_fusion.2.o1), channel_id=1, source_target_pairs={{0,8},{1,25},{2,10},{3,27},{4,12},{5,29},{6,14},{7,31},{8,16},{9,1... | collective-permute-start | bytes 4325384 | tf_op jit(solution)/shard_map/ppermute | solution.py:37
  73.9 20.3 %collective-permute-start.14 = (bf16[4,4,176,256]{3,2,1,0:T(8,128)(2,1)S(1)}, bf16[4,4,176,256]{3,2,1,0:T(8,128)(2,1)S(1)}, u32[]{:S(2)}, u32[]{:S(2)}) collective-permute-start(bf16[4,4,176,256]{3,2,1,0:T(8,128)(2,1)S(1)} %pad_maximum_fusion.3.o2), channel_id=1, source_target_pairs={{0,1},{1,0},{2,3},{3,2},{4,5},{5,4},{6,7},{7,6},{8,9},{9,8},{10,11... | collective-permute-start | bytes 4325384 | tf_op jit(solution)/shard_map/ppermute | solution.py:41
  77.2 20.3 %collective-permute-start.17 = (bf16[4,4,176,256]{3,2,1,0:T(8,128)(2,1)S(1)}, bf16[4,4,176,256]{3,2,1,0:T(8,128)(2,1)}, u32[]{:S(2)}, u32[]{:S(2)}) collective-permute-start(bf16[4,4,176,256]{3,2,1,0:T(8,128)(2,1)S(1)} %pad_maximum_fusion.3.o2), channel_id=1, source_target_pairs={{0,2},{1,7},{2,4},{3,1},{4,6},{5,3},{6,0},{7,5},{8,10},{9,15},{10,... | collective-permute-start | bytes 4325384 | tf_op jit(solution)/shard_map/ppermute | solution.py:37
  92.4 20.3 %collective-permute-start.21 = (bf16[4,4,176,256]{3,2,1,0:T(8,128)(2,1)S(1)}, bf16[4,4,176,256]{3,2,1,0:T(8,128)(2,1)}, u32[]{:S(2)}, u32[]{:S(2)}) collective-permute-start(bf16[4,4,176,256]{3,2,1,0:T(8,128)(2,1)S(1)} %collective-permute-done.15.o0), channel_id=1, source_target_pairs={{0,64},{1,97},{2,66},{3,99},{4,68},{5,101},{6,70},{7,103},{8,72},{... | collective-permute-start | bytes 4325384 | tf_op jit(solution)/shard_map/ppermute | solution.py:37
  94.1 18.6 %collective-permute-start.19 = (bf16[4,4,176,256]{3,2,1,0:T(8,128)(2,1)S(1)}, bf16[4,4,176,256]{3,2,1,0:T(8,128)(2,1)S(1)}, u32[]{:S(2)}, u32[]{:S(2)}) collective-permute-start(bf16[4,4,176,256]{3,2,1,0:T(8,128)(2,1)S(1)} %collective-permute-done.16.o1), channel_id=1, source_target_pairs={{0,1},{1,0},{2,3},{3,2},{4,5},{5,4},{6,7},{7,6},{8,9},{9,8},{10,11... | collective-permute-start | bytes 4325384 | tf_op jit(solution)/shard_map/ppermute | solution.py:41
  95.3 20.3 %collective-permute-start.22 = (bf16[4,4,176,256]{3,2,1,0:T(8,128)(2,1)S(1)}, bf16[4,4,176,256]{3,2,1,0:T(8,128)(2,1)}, u32[]{:S(2)}, u32[]{:S(2)}) collective-permute-start(bf16[4,4,176,256]{3,2,1,0:T(8,128)(2,1)S(1)} %collective-permute-done.16.o1), channel_id=1, source_target_pairs={{0,8},{1,25},{2,10},{3,27},{4,12},{5,29},{6,14},{7,31},{8,16},{9,1... | collective-permute-start | bytes 4325384 | tf_op jit(solution)/shard_map/ppermute | solution.py:37
  97.5 20.5 %collective-permute-start.23 = (bf16[4,4,176,256]{3,2,1,0:T(8,128)(2,1)}, bf16[4,4,176,256]{3,2,1,0:T(8,128)(2,1)}, u32[]{:S(2)}, u32[]{:S(2)}) collective-permute-start(bf16[4,4,176,256]{3,2,1,0:T(8,128)(2,1)} %collective-permute-done.17.o2), channel_id=1, source_target_pairs={{0,2},{1,7},{2,4},{3,1},{4,6},{5,3},{6,0},{7,5},{8,10},{9,15},{10,... | collective-permute-start | bytes 4325384 | tf_op jit(solution)/shard_map/ppermute | solution.py:37
  98.7 21.0 %collective-permute-start.20 = (bf16[4,4,176,256]{3,2,1,0:T(8,128)(2,1)}, bf16[4,4,176,256]{3,2,1,0:T(8,128)(2,1)}, u32[]{:S(2)}, u32[]{:S(2)}) collective-permute-start(bf16[4,4,176,256]{3,2,1,0:T(8,128)(2,1)} %collective-permute-done.17.o2), channel_id=1, source_target_pairs={{0,1},{1,0},{2,3},{3,2},{4,5},{5,4},{6,7},{7,6},{8,9},{9,8},{10,11... | collective-permute-start | bytes 4325384 | tf_op jit(solution)/shard_map/ppermute | solution.py:41
  113.9 20.5 %collective-permute-start.27 = (bf16[4,4,176,256]{3,2,1,0:T(8,128)(2,1)}, bf16[4,4,176,256]{3,2,1,0:T(8,128)(2,1)}, u32[]{:S(2)}, u32[]{:S(2)}) collective-permute-start(bf16[4,4,176,256]{3,2,1,0:T(8,128)(2,1)} %collective-permute-done.21.o0), channel_id=1, source_target_pairs={{0,64},{1,97},{2,66},{3,99},{4,68},{5,101},{6,70},{7,103},{8,72},{... | collective-permute-start | bytes 4325384 | tf_op jit(solution)/shard_map/ppermute | solution.py:37
  115.6 20.5 %collective-permute-start.28 = (bf16[4,4,176,256]{3,2,1,0:T(8,128)(2,1)}, bf16[4,4,176,256]{3,2,1,0:T(8,128)(2,1)}, u32[]{:S(2)}, u32[]{:S(2)}) collective-permute-start(bf16[4,4,176,256]{3,2,1,0:T(8,128)(2,1)} %collective-permute-done.22.o1), channel_id=1, source_target_pairs={{0,8},{1,25},{2,10},{3,27},{4,12},{5,29},{6,14},{7,31},{8,16},{9,1... | collective-permute-start | bytes 4325384 | tf_op jit(solution)/shard_map/ppermute | solution.py:37
  118.0 20.7 %collective-permute-start.29 = (bf16[4,4,176,256]{3,2,1,0:T(8,128)(2,1)}, bf16[4,4,176,256]{3,2,1,0:T(8,128)(2,1)}, u32[]{:S(2)}, u32[]{:S(2)}) collective-permute-start(bf16[4,4,176,256]{3,2,1,0:T(8,128)(2,1)} %collective-permute-done.23.o2), channel_id=1, source_target_pairs={{0,2},{1,7},{2,4},{3,1},{4,6},{5,3},{6,0},{7,5},{8,10},{9,15},{10,... | collective-permute-start | bytes 4325384 | tf_op jit(solution)/shard_map/ppermute | solution.py:37
  119.6 57.2 %collective-permute-start.25 = (bf16[4,4,176,256]{3,2,1,0:T(8,128)(2,1)}, bf16[4,4,176,256]{3,2,1,0:T(8,128)(2,1)}, u32[]{:S(2)}, u32[]{:S(2)}) collective-permute-start(bf16[4,4,176,256]{3,2,1,0:T(8,128)(2,1)} %collective-permute-done.22.o1), channel_id=1, source_target_pairs={{0,1},{1,0},{2,3},{3,2},{4,5},{5,4},{6,7},{7,6},{8,9},{9,8},{10,11... | collective-permute-start | bytes 4325384 | tf_op jit(solution)/shard_map/ppermute | solution.py:41
  119.7 57.1 %collective-permute-start.26 = (bf16[4,4,176,256]{3,2,1,0:T(8,128)(2,1)}, bf16[4,4,176,256]{3,2,1,0:T(8,128)(2,1)}, u32[]{:S(2)}, u32[]{:S(2)}) collective-permute-start(bf16[4,4,176,256]{3,2,1,0:T(8,128)(2,1)} %collective-permute-done.23.o2), channel_id=1, source_target_pairs={{0,1},{1,0},{2,3},{3,2},{4,5},{5,4},{6,7},{7,6},{8,9},{9,8},{10,11... | collective-permute-start | bytes 4325384 | tf_op jit(solution)/shard_map/ppermute | solution.py:41
  134.4 59.8 %collective-permute-start.30 = (bf16[4,4,176,256]{3,2,1,0:T(8,128)(2,1)}, bf16[4,4,176,256]{3,2,1,0:T(8,128)(2,1)}, u32[]{:S(2)}, u32[]{:S(2)}) collective-permute-start(bf16[4,4,176,256]{3,2,1,0:T(8,128)(2,1)} %collective-permute-done.27.o0), channel_id=1, source_target_pairs={{0,1},{1,0},{2,3},{3,2},{4,5},{5,4},{6,7},{7,6},{8,9},{9,8},{10,11... | collective-permute-start | bytes 4325384 | tf_op jit(solution)/shard_map/ppermute | solution.py:41
  136.1 58.0 %collective-permute-start.31 = (bf16[4,4,176,256]{3,2,1,0:T(8,128)(2,1)}, bf16[4,4,176,256]{3,2,1,0:T(8,128)(2,1)}, u32[]{:S(2)}, u32[]{:S(2)}) collective-permute-start(bf16[4,4,176,256]{3,2,1,0:T(8,128)(2,1)} %collective-permute-done.28.o1), channel_id=1, source_target_pairs={{0,1},{1,0},{2,3},{3,2},{4,5},{5,4},{6,7},{7,6},{8,9},{9,8},{10,11... | collective-permute-start | bytes 4325384 | tf_op jit(solution)/shard_map/ppermute | solution.py:41
  138.7 55.5 %collective-permute-start.32 = (bf16[4,4,176,256]{3,2,1,0:T(8,128)(2,1)}, bf16[4,4,176,256]{3,2,1,0:T(8,128)(2,1)}, u32[]{:S(2)}, u32[]{:S(2)}) collective-permute-start(bf16[4,4,176,256]{3,2,1,0:T(8,128)(2,1)} %collective-permute-done.29.o2), channel_id=1, source_target_pairs={{0,1},{1,0},{2,3},{3,2},{4,5},{5,4},{6,7},{7,6},{8,9},{9,8},{10,11... | collective-permute-start | bytes 4325384 | tf_op jit(solution)/shard_map/ppermute | solution.py:41
  208.8 201.5 %all-gather.5.cloned.1.call-start = ((), (), s32[]{:S(2)}) async-start(), calls=%async_computation | async-start | bytes 8519680 | tf_op jit(solution)/shard_map/cond/branch_0_fun/all_gather | solution.py:366
  209.7 248.0 %all-gather.7.cloned.1.call-start = ((), (), s32[]{:S(2)}) async-start(), calls=%async_computation.1 | async-start | bytes 8519680 | tf_op jit(solution)/shard_map/cond/branch_0_fun/all_gather | solution.py:367
  (88 other events, 579.7 us)
Sparse Core Ops, SparseCore 0:
  212.6 143.2 all-gather.4
  358.7 98.9 all-gather.6

commit v2 on v1

v2 whole, which is shorter than its diff:
```python
import functools
import math

import jax
import jax.numpy as jnp
from jax import lax
from jax.experimental import pallas as pl
from jax.experimental.pallas import tpu as pltpu
from jax.sharding import PartitionSpec as P

HD = 128
TOK = 128
SEG = 48
ROWS = TOK + SEG
AX = ("loop", "blk")
ROTS = ("xyz", "yzx", "zxy")
LEAD = (0, 1, 0)
SCALE = 1.0 / math.sqrt(HD)
LOG2 = math.log2(math.e) * SCALE
NEG = -1e30
BIG = 1 << 30
LIMIT = 100.0
VMEM = 48 * 2**20


def index(x, y, z, c):
    return (z % 2) * 64 + (((z // 2) * 4 + x) * 4 + y) * 2 + c


def moved(value, dim, rule):
    at = "xyz".index(dim)
    route = []
    for flat in range(128):
        c, y, x, z = flat % 2, flat // 2 % 4, flat // 8 % 4, flat // 32
        there = [x, y, z]
        there[at] = rule(there[at], c) % 4
        route.append((index(x, y, z, c), index(*there, c)))
    return lax.ppermute(value, AX, route)


def swapped(value):
    return lax.ppermute(value, AX, [(i, i ^ 1) for i in range(128)])


def tied(values):
    return list(lax.optimization_barrier(tuple(values)))


def dot_nt(a, b):
    return lax.dot_general(a, b, (((1,), (1,)), ((), ())), preferred_element_type=jnp.float32)


def dot_nn(a, b):
    return lax.dot_general(a, b, (((1,), (0,)), ((), ())), preferred_element_type=jnp.float32)


def lane_sums(w):
    total = w[:, :128]
    for at in range(128, w.shape[1], 128):
        total = total + w[:, at : at + 128]
    return total


def positions(bases, n, live):
    it = lax.broadcasted_iota(jnp.int32, (1, len(bases) * n), 1)
    pos = it + bases[0]
    inside = it
    for s in range(1, len(bases)):
        pos = jnp.where(it >= s * n, it + (bases[s] - s * n), pos)
        inside = jnp.where(it >= s * n, it - s * n, inside)
    return jnp.where(inside < live, pos, BIG)


def pack_kernel(keys, values, q, dq, nk, *pieces):
    ones = jnp.ones((HD, HD), jnp.bfloat16)

    def squares(ref):
        best = jnp.zeros((1, HD), jnp.float32)
        for at in range(0, ref.shape[1], HD):
            part = ref[:, at : at + HD].astype(jnp.float32)
            total = dot_nn((part * part).astype(jnp.bfloat16), ones)
            best = jnp.maximum(best, jnp.max(total, axis=0, keepdims=True))
        return best

    for r, piece in enumerate(pieces):
        live = min(SEG, TOK - SEG * r)
        for half, ref in enumerate((keys, values)):
            lanes = slice(half * HD, (half + 1) * HD)
            piece[0:TOK, lanes] = ref[:, r * HD : (r + 1) * HD]
            piece[TOK : TOK + live, lanes] = ref[SEG * r : SEG * r + live, 3 * HD : 4 * HD]
    for half, best in enumerate(
        (jnp.maximum(squares(keys), squares(nk)), jnp.maximum(squares(q), squares(dq)))
    ):
        bound = jnp.broadcast_to(jnp.sqrt(best) * 1.02, (16, HD))
        pieces[2][TOK + 32 : ROWS, half * HD : (half + 1) * HD] = bound.astype(jnp.bfloat16)


def pack(keys, values, q, dq, nk):
    vmem = pl.BlockSpec(memory_space=pltpu.VMEM)
    return pl.pallas_call(
        pack_kernel,
        out_shape=[jax.ShapeDtypeStruct((ROWS, 256), jnp.bfloat16)] * 3,
        in_specs=[vmem] * 5,
        out_specs=[vmem] * 3,
        compiler_params=pltpu.CompilerParams(vmem_limit_bytes=16 * 2**20),
        name="pack",
    )(keys, values, q, dq, nk)


def stage_kernel(t, meta, lens, q, dq, *rest):
    sides = [side for side, on in enumerate((t < 4, t > 0)) if on]
    first, last = t == 0, t == 4
    count = 3 * len(sides)
    sources, rest = rest[:count], rest[count:]
    if first:
        (nk, nv), accs_in, rest = rest[:2], (), rest[2:]
    else:
        accs_in, rest = rest[:4], rest[5:]
    if last:
        (pout, dout, handed, mx), rest = rest[:4], rest[4:]
    else:
        accs_out, handed, mx, rest = rest[:4], rest[4], rest[5], rest[6:]
    buf, spare, sp, sl, dp, dl, load_sem, spare_sem, acc_sem, out_sem, hand_sem = rest
    accs = (sp, sl, dp, dl)
    px, py, pz, core, match = meta[0], meta[1], meta[2], meta[3], meta[4]
    mine = (((pz >> 1) * 4 + px) * 4 + py) * 2 + core
    same = match == (pz & 1)

    near = t % 2
    active = jnp.where(same, near, 1 - near)

    def load(r, side, part):
        source = sources[3 * sides.index(side) + r]
        if part is None:
            return pltpu.make_async_copy(source, buf.at[r, side], load_sem.at[r, side, 0])
        lead, n = ((0, 1), (3, 1), (1, 2))[part]
        span = pl.ds(lead, n)
        return pltpu.make_async_copy(
            source.at[span], buf.at[r, side, span], load_sem.at[r, side, part]
        )

    acc_loads = {
        (head, i): pltpu.make_async_copy(
            accs_in[i].at[head], accs[i].at[head], acc_sem.at[head, i]
        )
        for head in (1, 2, 0, 3)
        for i in range(0 if first else 4)
    }
    needed = {1: [], 2: [], 0: []}
    for r in (1, 2):
        needed[r] = [load(r, side, part) for part in range(2) for side in sides]
    if near in sides:
        needed[0] = [load(0, near, None)]
    others = [load(r, side, 2) for r in (1, 2) for side in sides]
    if 1 - near in sides:
        others.append(load(0, 1 - near, None))
    for r in (1, 2, 0):
        for copy in needed[r]:
            copy.start()
        if not first:
            for i in range(2):
                acc_loads[r, i].start()
    if not first:
        for i in range(2):
            acc_loads[3, i].start()

    @pl.when(jnp.logical_not(same))
    def _():
        for copy in others:
            copy.start()

    spares = [
        pltpu.make_async_copy(
            sources[3 * sides.index(side) + 2].at[:, :, pl.ds(TOK + 32, 16), :],
            spare.at[side],
            spare_sem.at[side],
        )
        for side in sides
    ]
    if not first:
        for head in (1, 2, 0, 3):
            for i in range(2, 4):
                acc_loads[head, i].start()
    for copy in spares:
        copy.start()
    if first:
        sp[...] = jnp.zeros_like(sp)
        sl[...] = jnp.zeros_like(sl)

    def sided(side):
        if isinstance(side, int):
            return (core, t) if side == 0 else (1 - core, t - 1)
        return jnp.where(side == 0, core, 1 - core), jnp.where(side == 0, t, t - 1)

    def place(r, side, lead, inner):
        cs, stage = sided(side)

        def offset(i):
            return jnp.where(
                i == 0, 0, jnp.where(i == 3, 2, jnp.where(i == 1, 1 + 2 * cs, 3 - 2 * cs))
            )

        turn = stage * (2 * cs - 1)
        el, ei = offset(lead), offset(inner)
        x = jnp.where(r == 0, px ^ el, jnp.where(r == 1, (px + turn) & 3, px ^ ei))
        y = jnp.where(r == 2, (py + turn) & 3, py ^ ei)
        z = jnp.where(r == 0, (pz + turn) & 3, pz ^ el)
        return (((z >> 1) * 4 + x) * 4 + y) * 2 + cs

    def facing(lead):
        return jnp.where(lead == 1, 2, jnp.where(lead == 2, 1, lead))

    def led(side, i, own):
        far = 1 + i if side == 0 else 2 - i
        return jnp.where(own, 3 * i, far)

    def hand(r, act):
        live = min(SEG, TOK - SEG * r)

        def slots(side, lead):
            for inner in range(4):
                row = place(r, side, lead, inner) * TOK
                for half in range(2):
                    for lo, n, to, head in ((0, TOK, 0, r), (TOK, live, SEG * r, 3)):
                        act(
                            pltpu.make_async_copy(
                                buf.at[r, side, lead, inner, pl.ds(lo, n), pl.ds(half * HD, HD)],
                                handed.at[
                                    half,
                                    pl.ds(pl.multiple_of(row + to, 16), n),
                                    pl.ds(head * HD, HD),
                                ],
                                hand_sem,
                            )
                        )

        if r == 0:

            def some(i, _):
                slots(active, i)
                return 0

            @pl.when(usable)
            def _():
                lax.fori_loop(0, 4, some, 0)

        else:

            def some(i, _):
                for side in sides:
                    slots(side, led(side, i, same))
                return 0

            lax.fori_loop(0, 2, some, 0)

    usable = True if len(sides) == 2 else active == sides[0]
    prompt_usable = len(sides) == 2 or near == sides[0]

    def gathered(r, groups, lo, n, base, live):
        keys, bases = [], []
        for side, lead in groups:
            keys.append(buf[r, side, lead, :, lo : lo + n, :].reshape(4 * n, 256))
            bases += [place(r, side, lead, inner) * TOK + base for inner in range(4)]
        return jnp.concatenate(keys, 0), bases, n, live

    def groups_of(r, i, own):
        if r == 0:
            side = near if own is True else active
            return [(side, 2 * i), (side, 2 * i + 1)]
        if len(sides) == 2:
            return [(side, led(side, i, own)) for side in sides]
        return [(sides[0], led(sides[0], j, own)) for j in range(2)]

    def main_tile(r, i, own):
        return gathered(r, groups_of(r, i, own), 0, TOK, 0, TOK)

    def third_tile(r, i, own):
        if r == 0:
            side = near if own is True else active
            groups = [(side, j) for j in range(4)]
        else:
            groups = [(side, led(side, j, own)) for j in range(2) for side in sides]
        return gathered(r, groups, TOK, SEG, SEG * r, min(SEG, TOK - SEG * r))

    def queries_of(head):
        return jnp.concatenate(
            [q[:, (head * 8 + g) * HD : (head * 8 + g + 1) * HD] for g in range(8)], 0
        )

    def prompt_add(head, s, v):
        w = jnp.exp2(s)
        sl[head] += jnp.sum(w.reshape(-1, 8, 1024), axis=0)
        sp[head] += dot_nn(jnp.transpose(v), w.astype(jnp.bfloat16))

    def prompt_tile(head, kv, bases, n, live):
        @pl.when(functools.reduce(jnp.minimum, bases) < mine * TOK)
        def _():
            row = lax.broadcasted_iota(jnp.int32, (n, HD), 0)
            lane = lax.broadcasted_iota(jnp.int32, (n, HD), 1)
            hidden = jnp.concatenate(
                [
                    jnp.where(
                        (lane == 0) & ((row >= live) | (base >= mine * TOK)), NEG, 0.0
                    ).astype(jnp.bfloat16)
                    for base in bases
                ],
                0,
            )
            unit = lax.broadcasted_iota(jnp.int32, (1024, HD), 1) == 0
            qs = jnp.concatenate(
                [queries_of(head), unit.astype(jnp.float32).astype(jnp.bfloat16)], 1
            )
            ks = jnp.concatenate([kv[:, :HD], hidden], 1)
            prompt_add(head, dot_nt(ks, qs) * LOG2, kv[:, HD:])

    def decode_tile(head, kv, bases, n, live):
        k, v = kv[:, :HD], kv[:, HD:]
        pos = positions(bases, n, live)
        limit = jnp.concatenate([lens[:, 0:1]] * 4, 0)
        for chunk in range(2):
            rows = slice(chunk * 256, chunk * 256 + 256)
            at = head * 8 + 4 * chunk
            part = [dq[:, g * HD : (g + 1) * HD] for g in range(at, at + 4)]
            s = dot_nt(jnp.concatenate(part, 0), k) * LOG2
            w = jnp.exp2(jnp.where(pos < limit, s, NEG))
            dl[head, rows, :] += lane_sums(w)
            dp[head, rows, :] += dot_nn(w.astype(jnp.bfloat16), v)

    def own_block(head):
        row = lax.broadcasted_iota(jnp.int32, (TOK, 1024), 0)
        col = lax.broadcasted_iota(jnp.int32, (TOK, 1024), 1) % TOK
        if head < 3:
            kv = buf[head, 0, 0, 0, 0:TOK, :]
        else:
            kv = jnp.concatenate(
                [
                    buf[r, 0, 0, 0, TOK : TOK + min(SEG, TOK - SEG * r), :]
                    for r in range(3)
                ],
                0,
            )
        s = dot_nt(kv[:, :HD], queries_of(head)) * LOG2
        prompt_add(head, jnp.where(row <= col, s, NEG), kv[:, HD:])

    def fresh(head):
        lanes = slice(head * HD, (head + 1) * HD)
        step = lax.broadcasted_iota(jnp.int32, (64, 1), 0) >= 32
        for g in range(8):
            at = (head * 8 + g) * HD
            query = dq[:, at : at + HD].astype(jnp.float32)
            acc = total = 0.0
            for j in range(2):
                rows = slice(32 * j, 32 * j + 32)
                key = jnp.concatenate([nk[rows, lanes]] * 2, 0).astype(jnp.float32)
                value = jnp.concatenate([nv[rows, lanes]] * 2, 0).astype(jnp.float32)
                s = jnp.sum(query * key, axis=1, keepdims=True) * LOG2
                w = jnp.exp2(s if j == 0 else jnp.where(step, s, NEG))
                total = total + w
                acc = acc + w.astype(jnp.bfloat16).astype(jnp.float32) * value
            rows = slice(g * 64, g * 64 + 64)
            dp[head, rows, :] = acc
            dl[head, rows, :] = jnp.broadcast_to(total / HD, (64, HD))

    def finish_prompt(head):
        out = sp[head] / jnp.sum(sl[head], axis=0, keepdims=True)
        for g in range(8):
            lanes = slice((head * 8 + g) * HD, (head * 8 + g + 1) * HD)
            part = jnp.transpose(out[:, g * TOK : (g + 1) * TOK])
            pout[:, lanes] = part.astype(jnp.bfloat16)

    def finish_decode(head):
        for g in range(8):
            lanes = slice((head * 8 + g) * HD, (head * 8 + g + 1) * HD)
            rows = slice(g * 64, (g + 1) * 64)
            total = jnp.sum(dl[head, rows, :], axis=1, keepdims=True)
            dout[:, lanes] = (dp[head, rows, :] / total).astype(jnp.bfloat16)

    stores = []

    def settle(head, which):
        if last:
            (finish_decode if which else finish_prompt)(head)
            return
        for i in range(2 * which, 2 * which + 2):
            copy = pltpu.make_async_copy(
                accs[i].at[head], accs_out[i].at[head], out_sem.at[head, i]
            )
            copy.start()
            stores.append(copy)

    def loop(count, work):
        def one(i, _):
            work(i)
            return 0

        lax.fori_loop(0, count, one, 0)

    def when(condition, work):
        if condition is True:
            work()
        elif condition is not False:
            pl.when(condition)(work)

    def tiles(r):
        return 2 if r == 0 or len(sides) == 2 else 1

    for r in (1, 2, 0):
        for copy in needed[r]:
            copy.wait()
        if first:
            own_block(r)
        else:
            for i in range(2):
                acc_loads[r, i].wait()
        if r != 0 or prompt_usable:
            loop(tiles(r), lambda i, r=r: prompt_tile(r, *main_tile(r, i, True)))
        settle(r, 0)
    if first:
        own_block(3)
    else:
        for i in range(2):
            acc_loads[3, i].wait()
    for r in (1, 2, 0):
        if r != 0 or prompt_usable:
            prompt_tile(3, *third_tile(r, 0, True))
    settle(3, 0)

    @pl.when(jnp.logical_not(same))
    def _():
        for copy in others:
            copy.wait()

    for r in (1, 2, 0):
        hand(r, lambda copy: copy.start())
    for r in (1, 2, 0):
        if first:
            fresh(r)
        else:
            for i in range(2, 4):
                acc_loads[r, i].wait()
        when(
            True if r else usable,
            lambda r=r: loop(
                tiles(r), lambda i: decode_tile(r, *main_tile(r, i, same))
            ),
        )
        settle(r, 1)
    if first:
        fresh(3)
    else:
        for i in range(2, 4):
            acc_loads[3, i].wait()
    for r in (1, 2, 0):
        when(
            True if r else usable, lambda r=r: decode_tile(3, *third_tile(r, 0, same))
        )
    settle(3, 1)

    high = jnp.zeros((16, 256), jnp.float32)
    for side, copy in zip(sides, spares):
        copy.wait()
        part = spare[side].reshape(16, 16, 256).astype(jnp.float32)
        high = jnp.maximum(high, jnp.max(part, axis=0))
    mx[...] = high
    for copy in stores:
        copy.wait()
    for r in (1, 2, 0):
        hand(r, lambda copy: copy.wait())


def run_stage(t, meta, lens, q, dq, sources, accs, handed, fresh):
    anywhere = pl.BlockSpec(memory_space=pl.ANY)
    vmem = pl.BlockSpec(memory_space=pltpu.VMEM)
    acc_shapes = [
        jax.ShapeDtypeStruct(shape, jnp.float32)
        for shape in ((4, HD, 1024), (4, 8, 1024), (4, 512, HD), (4, 512, HD))
    ]
    handed_shape = jax.ShapeDtypeStruct((2, 8192, 512), jnp.bfloat16)
    mx_shape = jax.ShapeDtypeStruct((16, 256), jnp.float32)
    carried = [] if t == 0 else [*accs, handed]
    new = [*fresh] if t == 0 else []
    at = 4 + len(sources)
    if t == 4:
        outs = [
            jax.ShapeDtypeStruct(q.shape, jnp.bfloat16),
            jax.ShapeDtypeStruct(dq.shape, jnp.bfloat16),
            handed_shape,
            mx_shape,
        ]
        specs = [vmem, vmem, anywhere, vmem]
        alias = {at + 4: 2}
    else:
        outs = [*acc_shapes, handed_shape, mx_shape]
        specs = [anywhere] * 5 + [vmem]
        alias = {} if t == 0 else {at + i: i for i in range(5)}
    work = 16 * HD * len(sources) // 3 * 6144
    return pl.pallas_call(
        functools.partial(stage_kernel, t),
        out_shape=outs,
        in_specs=[pl.BlockSpec(memory_space=pltpu.SMEM), vmem, vmem, vmem]
        + [anywhere] * (len(sources) + len(carried))
        + [vmem] * len(new),
        out_specs=specs,
        input_output_aliases=alias,
        scratch_shapes=[
            pltpu.VMEM((3, 2, 4, 4, ROWS, 256), jnp.bfloat16),
            pltpu.VMEM((2, 4, 4, 16, 256), jnp.bfloat16),
            pltpu.VMEM((4, HD, 1024), jnp.float32),
            pltpu.VMEM((4, 8, 1024), jnp.float32),
            pltpu.VMEM((4, 512, HD), jnp.float32),
            pltpu.VMEM((4, 512, HD), jnp.float32),
            pltpu.SemaphoreType.DMA((3, 2, 3)),
            pltpu.SemaphoreType.DMA((2,)),
            pltpu.SemaphoreType.DMA((4, 4)),
            pltpu.SemaphoreType.DMA((4, 4)),
            pltpu.SemaphoreType.DMA,
        ],
        compiler_params=pltpu.CompilerParams(vmem_limit_bytes=VMEM),
        cost_estimate=pl.CostEstimate(
            flops=work * 512, bytes_accessed=30 << 20, transcendentals=work
        ),
        name=f"stage{t}",
    )(meta, lens, q, dq, *sources, *carried, *new)


def careful(queries, keys, values, handed, dec_queries, new_keys, new_values, row_len):
    place = lax.axis_index("blk")
    tok, block = TOK, 512
    count = lax.axis_size("blk")
    seq = count * tok
    right = [(i, (i + 1) % count) for i in range(count)]

    def collect(i, carry):
        shard, cache = carry
        cache = lax.dynamic_update_slice(cache, shard, (0, (place - i) % count * tok, 0))
        return lax.ppermute(shard, "blk", right), cache

    shard = jnp.stack([keys[0], values[0]])
    cache = jnp.zeros((2, seq, 512), jnp.bfloat16)
    _, cache = lax.fori_loop(0, count, collect, (shard, cache))
    all_k = cache[0].reshape(seq, 4, HD)
    all_v = cache[1].reshape(seq, 4, HD)

    def attend(query, cache_k, cache_v, limit, state):
        def turn(i, state):
            big, total, acc = state
            part_k = lax.dynamic_slice_in_dim(cache_k, i * block, block, 0)
            part_v = lax.dynamic_slice_in_dim(cache_v, i * block, block, 0)
            s = jnp.einsum("tkgd,skd->kgts", query, part_k, preferred_element_type=jnp.float32)
            s = s * SCALE
            allow = (i * block + jnp.arange(block))[None, :] < limit[:, None]
            s = jnp.where(allow, s, NEG)
            top = jnp.maximum(big, jnp.max(s, axis=-1))
            w = jnp.where(allow, jnp.exp(s - top[..., None]), 0.0)
            shrink = jnp.exp(big - top)
            total = total * shrink + jnp.sum(w, axis=-1)
            acc = acc * shrink[..., None] + jnp.einsum(
                "kgts,skd->kgtd",
                w.astype(jnp.bfloat16),
                part_v,
                preferred_element_type=jnp.float32,
            )
            return top, total, acc

        return lax.fori_loop(0, seq // block, turn, state)

    def finish(state, rows):
        out = state[2] / state[1][..., None]
        return out.transpose(2, 0, 1, 3).reshape(rows, 4096).astype(jnp.bfloat16)

    state = (
        jnp.full((4, 8, tok), NEG, jnp.float32),
        jnp.zeros((4, 8, tok), jnp.float32),
        jnp.zeros((4, 8, tok, HD), jnp.float32),
    )
    limit = place * tok + jnp.arange(tok) + 1
    state = attend(queries[0].reshape(tok, 4, 8, HD), all_k, all_v, limit, state)
    prompt_out = finish(state, tok)

    steps, rows = dec_queries.shape[:2]
    cache_k = handed[0].reshape(seq, 4, HD)
    cache_v = handed[1].reshape(seq, 4, HD)
    outs = []
    for step in range(steps):
        dquery = dec_queries[step].reshape(rows, 4, 8, HD)
        nk = new_keys[: step + 1].reshape(step + 1, rows, 4, HD)
        nv = new_values[: step + 1].reshape(step + 1, rows, 4, HD)
        s = jnp.einsum("rkgd,jrkd->kgrj", dquery, nk, preferred_element_type=jnp.float32) * SCALE
        top = jnp.max(s, axis=-1)
        w = jnp.exp(s - top[..., None])
        acc = jnp.einsum(
            "kgrj,jrkd->kgrd", w.astype(jnp.bfloat16), nv, preferred_element_type=jnp.float32
        )
        state = attend(dquery, cache_k, cache_v, row_len, (top, jnp.sum(w, axis=-1), acc))
        outs.append(finish(state, rows))
    return prompt_out, jnp.stack(outs)


def body(queries, keys, values, match, dec_queries, new_keys, new_values, row_len):
    flat = lax.axis_index("loop") * 64 + lax.axis_index("blk")
    core, y, x = flat % 2, flat // 2 % 4, flat // 8 % 4
    z = flat // 32 % 2 * 2 + flat // 64
    meta = jnp.stack([x, y, z, core, match[0], 0, 0, 0]).astype(jnp.int32)
    q, dq = queries[0], dec_queries.reshape(64, 4096)
    lens = jnp.broadcast_to(jnp.tile(row_len, 2)[:, None], (64, HD)).astype(jnp.int32)
    fresh = [v.reshape(64, 512) for v in (new_keys, new_values)]

    pieces = pack(keys[0], values[0], q, dq, fresh[0])
    pieces = tied([p[None, None] for p in pieces])
    for phase in range(2):
        for step in range(2):
            got = [
                moved(p, rot[phase], lambda a, c: a ^ (1 if step == c else 3))
                for p, rot in zip(pieces, ROTS)
            ]
            got = tied(got)
            axes = [lead if phase == 0 else 1 - lead for lead in LEAD]
            pieces = tied(
                [jnp.concatenate([p, g], a) for p, g, a in zip(pieces, got, axes)]
            )

    accs, handed, sib, high = [], None, [], []
    for t in range(5):
        across = [swapped(p) for p in pieces]
        onward = []
        if t < 3:
            across[0], held = tied([across[0], pieces[2]])
            onward = [
                moved(p, rot[2], lambda a, c: a + 1 - 2 * c)
                for p, rot in zip([pieces[0], pieces[1], held], ROTS)
            ]
        res = run_stage(t, meta, lens, q, dq, [*pieces, *sib], accs, handed, fresh)
        if t < 4:
            accs, handed = res[:4], res[4]
            ready = tied([*onward, *across, *accs, handed])
            pieces, ready = ready[: len(onward)], ready[len(onward) :]
            sib, accs, handed = ready[:3], ready[3:7], ready[7]
        else:
            prompt_out, dec_out, handed = res[:3]
        high.append(res[-1])
    high = functools.reduce(jnp.maximum, high)
    bound = jnp.max(high[:, :HD]) * jnp.max(high[:, HD:]) * LOG2
    prompt_out, dec_out = lax.cond(
        bound < LIMIT,
        lambda: (prompt_out, dec_out.reshape(dec_queries.shape)),
        lambda: careful(
            queries, keys, values, handed, dec_queries, new_keys, new_values, row_len
        ),
    )
    return prompt_out[None], handed[None], dec_out


def solution(mesh):
    in_specs = (
        P("loop", "blk", None),
        P("loop", "blk", None),
        P("loop", "blk", None),
        P(("loop", "blk")),
        P(None, ("loop", "blk"), None),
        P(None, ("loop", "blk"), None),
        P(None, ("loop", "blk"), None),
        P(("loop", "blk")),
    )
    out_specs = (
        P("loop", "blk", None),
        P(("loop", "blk"), None, None, None),
        P(None, ("loop", "blk"), None),
    )
    return jax.shard_map(body, mesh=mesh, in_specs=in_specs, out_specs=out_specs, check_vma=False)
```

time: 761 us -> 1380 us (1.81)
  waiting for transfers between devices: 122 us -> 727 us
  local copies, waits for them, and re-layouts: 128 us -> 160 us
  between operations: 19.6 us -> 3.08 us
  starting transfers between devices: 27.4 us -> 41.7 us
    ppermute x0 -> x64, waiting for transfers between devices: none -> 678 us  [collect(): return (lax.ppermute(shard, 'blk', right), cache)]
    dynamic_update_slice x0 -> x128, local copies, waits for them, and re-layouts: none -> 59.3 us  [collect(): lax.dynamic_update_slice(cache, shard, (0, (place - i) % count * tok, 0))]
    all_gather x2 -> x0, waiting for transfers between devices: 47.4 us -> none  [the longest x1 47.4 us: careful(): all_v = lax.all_gather(values[0], 'blk', tiled=True).reshape(-1, 4, HD)]
    ppermute x21, waiting for transfers between devices: 74.2 us -> 47.2 us  [moved(): return lax.ppermute(value, AX, route)]
    while x144 -> x80, local copies, waits for them, and re-layouts: 39 us -> 18.3 us
    another operation x7 -> x70, local copies, waits for them, and re-layouts: 23.6 us -> 29 us
    pallas_call x4 -> x6, Pallas kernels: 57.8 us -> 55.9 us  [the longest x5 53.6 us: run_stage(): pl.pallas_call(functools.partial(stage_kernel, t), out_shape=outs, in_spe...]
  transfers between devices with their start and end apart: 35 -> 97, of which waited for: 18 -> 83; matrix products, arithmetic and copies ran while one was open for 28% -> 4% of each run, Pallas kernels for 6% -> 3%
where the time goes in v2:
time: 1380 us; the launch traced here: 1370 us
  waiting for transfers between devices  727 us (53%)
  matrix products  269 us (19%)
  local copies, waits for them, and re-layouts  160 us (12%)
  other arithmetic  107 us (8%)
  Pallas kernels  55.9 us (4%)
  starting transfers between devices  41.7 us (3%)
    ppermute x64, waiting for transfers between devices, collect(): return (lax.ppermute(shard, 'blk', right), cache)  678 us
    dot_general x48, matrix products, turn(): jnp.einsum('tkgd,skd->kgts', query, part_k, preferred_element_type=jnp.fl...  143 us
    dot_general x48, matrix products, turn(): jnp.einsum('kgts,skd->kgtd', w.astype(jnp.bfloat16), part_v, preferred_el...  126 us
    reduce_sum x48, other arithmetic, turn(): total = total * shrink + jnp.sum(w, axis=-1)  95.8 us
    dynamic_update_slice x128, local copies, waits for them, and re-layouts, collect(): lax.dynamic_update_slice(cache, shard, (0, (place - i) % count * tok, 0))  59.3 us
    pallas_call x5, Pallas kernels, run_stage(): pl.pallas_call(functools.partial(stage_kernel, t), out_shape=outs, in_spe...  53.6 us
    ppermute x21, waiting for transfers between devices, moved(): return lax.ppermute(value, AX, route)  47.2 us
    another operation x70, local copies, waits for them, and re-layouts  29 us
  transfers between devices with their start and end apart: 97, of which 83 were waited for; matrix products, arithmetic and copies ran while one was open for 4% of the time, Pallas kernels for 3%

profile of v2, /device:TPU:0, one launch (start us, length us, event | category | flops | bytes accessed | tf_op | source)
XLA Modules:
  0.0 1370.3 jit_solution(11475546726226385306)
XLA Ops:
  56.2 10.8 stage0.1
  78.5 12.0 stage1.1
  103.5 11.2 stage2.1
  123.0 12.0 stage3.1
  145.9 1224.3 %conditional.1 = (bf16[2,32,4096]{2,1,0:T(8,128)(2,1)}, bf16[1,128,4096]{2,1,0:T(8,128)(2,1)}) conditional(s32[]{:T(128)} %convert_element_type.76, (bf16[2,32,512]{2,1,0:T(8,128)(2,1)S(1)}, bf16[2,32,4096]{2,1,0:T(8,128)(2,1)S(1)}, bf16[2,32,512]{2,1,0:T(8,128)(2,1)S(1)}, bf16[2,8192,512]{2,1,0:T(8,128)(2,1)}, s32[32]{0:T(128)S(1)}, ...), branch_computations={%region_2.19_spmd, %region_19.20_spmd} | conditional | flops 1657168640 | bytes 260901488 | solution.py:643
  147.2 21.2 %copy.82 = bf16[2,8192,512]{1,2,0:T(8,128)(2,1)} copy(bf16[2,8192,512]{2,1,0:T(8,128)(2,1)} %get-tuple-element.876) | data formatting | bytes 33554432 | tf_op jit(solution)/shard_map
  168.5 11.6 fusion.78
  180.1 12.0 copy.62
  192.1 11.9 copy.64
  204.1 68.5 %while.66 = (s32[]{:T(128)}, f32[4,8,32]{2,1,0:T(8,128)S(1)}, f32[4,8,32]{2,1,0:T(8,128)S(1)}, f32[4,8,32,128]{3,2,1,0:T(8,128)S(1)}, s32[32]{0:T(128)S(1)}, /*i...) while((s32[]{:T(128)}, f32[4,8,32]{2,1,0:T(8,128)S(1)}, ...), condition=%wide.region_12.12_spmd, body=%wide.region_9.11_spmd.sunk | while | flops 275532288 | bytes 8786223 | solution.py:565
  274.0 68.5 %while.65 = (s32[]{:T(128)}, f32[4,8,32]{2,1,0:T(8,128)S(1)}, f32[4,8,32]{2,1,0:T(8,128)S(1)}, f32[4,8,32,128]{3,2,1,0:T(8,128)S(1)}, s32[32]{0:T(128)S(1)}, /*i...) while((s32[]{:T(128)}, f32[4,8,32]{2,1,0:T(8,128)S(1)}, ...), condition=%wide.region_6.6_spmd, body=%wide.region_3.5_spmd.sunk | while | flops 275532288 | bytes 8786223 | solution.py:565
  349.8 750.1 %while.67 = (s32[]{:T(128)}, bf16[2,128,512]{2,1,0:T(8,128)(2,1)S(1)}, bf16[2,8192,512]{1,2,0:T(8,128)(2,1)}, s32[]{:T(128)}, s32[]{:T(128)}, /*index=5*/s32[]{:T(128)}, s32[]{:T(128)}, s32[]{:T(128)}, s32[]{:T(128)}, s32[]{:T(128)}) while((s32[]{:T(128)}, bf16[2,128,512]{2,1,0:T(8,128)(2,1)S(1)}, bf16[2,8192,512]{1,2,0:T(8,128)(2,1)}, ...), condition=%wide.region_14.14_spmd, body=%wide.region_13.13_spmd.sunk | while | flops 18 | bytes 2621752 | solution.py:540
  354.3 14.1 %collective-permute-done = bf16[2,128,512]{2,1,0:T(8,128)(2,1)S(1)} collective-permute-done((bf16[2,128,512]{2,1,0:T(8,128)(2,1)S(1)}, bf16[2,128,512]{2,1,0:T(8,128)(2,1)S(1)}, u32[]{:S(2)}, u32[]{:S(2)}) %collective-permute-start) | collective-permute-done | bytes 262176 | tf_op jit(solution)/shard_map/cond/branch_0_fun/while/body/eval_jaxpr/ppermute | solution.py:536
  648.1 10.6 collective-permute-done
  671.3 10.6 collective-permute-done
  682.9 10.6 collective-permute-done
  717.8 10.6 collective-permute-done
  729.4 10.6 collective-permute-done
  741.0 10.6 collective-permute-done
  822.3 10.6 collective-permute-done
  950.0 10.6 collective-permute-done
  984.9 10.6 collective-permute-done
  1099.9 11.6 fusion.77
  1112.9 254.5 %while.68 = (s32[]{:T(128)}, f32[4,8,128]{2,1,0:T(8,128)S(1)}, f32[4,8,128]{2,1,0:T(8,128)S(1)}, f32[4,8,128,128]{3,2,1,0:T(8,128)S(1)}, bf16[8192,4,128]{0,2,1:...) while((s32[]{:T(128)}, f32[4,8,128]{2,1,0:T(8,128)S(1)}, ...), condition=%wide.region_18.18_spmd.clone, body=%wide.region_15.17_spmd.clone.sunk | while | flops 1102664448 | bytes 65541336 | solution.py:565
  (906 shorter events, 1136.9 us)
Async XLA Ops:
  31.2 12.6 collective-permute-start.10
  31.8 12.5 collective-permute-start.11
  35.1 12.5 collective-permute-start.12
  49.2 20.4 %collective-permute-start.13 = (bf16[4,4,176,256]{3,2,1,0:T(8,128)(2,1)S(1)}, bf16[4,4,176,256]{3,2,1,0:T(8,128)(2,1)}, u32[]{:S(2)}, u32[]{:S(2)}) collective-permute-start(bf16[4,4,176,256]{3,2,1,0:T(8,128)(2,1)S(1)} %pad_maximum_fusion.2.rest_0_), channel_id=1, source_target_pairs={{0,64},{1,97},{2,66},{3,99},{4,68},{5,101},{6,70},{7,103},{8,72},{... | collective-permute-start | bytes 4325384 | tf_op jit(solution)/shard_map/ppermute | solution.py:38
  50.7 20.3 %collective-permute-start.14 = (bf16[4,4,176,256]{3,2,1,0:T(8,128)(2,1)S(1)}, bf16[4,4,176,256]{3,2,1,0:T(8,128)(2,1)}, u32[]{:S(2)}, u32[]{:S(2)}) collective-permute-start(bf16[4,4,176,256]{3,2,1,0:T(8,128)(2,1)S(1)} %pad_maximum_fusion.3.rest_1_), channel_id=1, source_target_pairs={{0,8},{1,25},{2,10},{3,27},{4,12},{5,29},{6,14},{7,31},{8,16},{9,1... | collective-permute-start | bytes 4325384 | tf_op jit(solution)/shard_map/ppermute | solution.py:38
  50.7 20.3 %collective-permute-start.17 = (bf16[4,4,176,256]{3,2,1,0:T(8,128)(2,1)S(1)}, bf16[4,4,176,256]{3,2,1,0:T(8,128)(2,1)}, u32[]{:S(2)}, u32[]{:S(2)}) collective-permute-start(bf16[4,4,176,256]{3,2,1,0:T(8,128)(2,1)S(1)} %pad_maximum_fusion.3.rest_1_), channel_id=1, source_target_pairs={{0,1},{1,0},{2,3},{3,2},{4,5},{5,4},{6,7},{7,6},{8,9},{9,8},{10,11... | collective-permute-start | bytes 4325384 | tf_op jit(solution)/shard_map/ppermute | solution.py:42
  50.7 20.3 %collective-permute-start.18 = (bf16[4,4,176,256]{3,2,1,0:T(8,128)(2,1)}, bf16[4,4,176,256]{3,2,1,0:T(8,128)(2,1)}, u32[]{:S(2)}, u32[]{:S(2)}) collective-permute-start(bf16[4,4,176,256]{3,2,1,0:T(8,128)(2,1)} %pad_maximum_fusion.4.rest_2_), channel_id=1, source_target_pairs={{0,1},{1,0},{2,3},{3,2},{4,5},{5,4},{6,7},{7,6},{8,9},{9,8},{10,11... | collective-permute-start | bytes 4325384 | tf_op jit(solution)/shard_map/ppermute | solution.py:42
  53.6 20.5 %collective-permute-start.16 = (bf16[4,4,176,256]{3,2,1,0:T(8,128)(2,1)}, bf16[4,4,176,256]{3,2,1,0:T(8,128)(2,1)}, u32[]{:S(2)}, u32[]{:S(2)}) collective-permute-start(bf16[4,4,176,256]{3,2,1,0:T(8,128)(2,1)} %pad_maximum_fusion.4.rest_2_), channel_id=1, source_target_pairs={{0,2},{1,7},{2,4},{3,1},{4,6},{5,3},{6,0},{7,5},{8,10},{9,15},{10,... | collective-permute-start | bytes 4325384 | tf_op jit(solution)/shard_map/ppermute | solution.py:38
  74.1 20.4 %collective-permute-start.19 = (bf16[4,4,176,256]{3,2,1,0:T(8,128)(2,1)}, bf16[4,4,176,256]{3,2,1,0:T(8,128)(2,1)S(1)}, u32[]{:S(2)}, u32[]{:S(2)}) collective-permute-start(bf16[4,4,176,256]{3,2,1,0:T(8,128)(2,1)} %collective-permute-done.13.rest_0_), channel_id=1, source_target_pairs={{0,64},{1,97},{2,66},{3,99},{4,68},{5,101},{6,70},{7,103},{8,72},{... | collective-permute-start | bytes 4325384 | tf_op jit(solution)/shard_map/ppermute | solution.py:38
  75.6 20.4 %collective-permute-start.20 = (bf16[4,4,176,256]{3,2,1,0:T(8,128)(2,1)}, bf16[4,4,176,256]{3,2,1,0:T(8,128)(2,1)S(1)}, u32[]{:S(2)}, u32[]{:S(2)}) collective-permute-start(bf16[4,4,176,256]{3,2,1,0:T(8,128)(2,1)} %collective-permute-done.14.rest_1_), channel_id=1, source_target_pairs={{0,8},{1,25},{2,10},{3,27},{4,12},{5,29},{6,14},{7,31},{8,16},{9,1... | collective-permute-start | bytes 4325384 | tf_op jit(solution)/shard_map/ppermute | solution.py:38
  75.6 20.4 %collective-permute-start.23 = (bf16[4,4,176,256]{3,2,1,0:T(8,128)(2,1)}, bf16[4,4,176,256]{3,2,1,0:T(8,128)(2,1)S(1)}, u32[]{:S(2)}, u32[]{:S(2)}) collective-permute-start(bf16[4,4,176,256]{3,2,1,0:T(8,128)(2,1)} %collective-permute-done.14.rest_1_), channel_id=1, source_target_pairs={{0,1},{1,0},{2,3},{3,2},{4,5},{5,4},{6,7},{7,6},{8,9},{9,8},{10,11... | collective-permute-start | bytes 4325384 | tf_op jit(solution)/shard_map/ppermute | solution.py:42
  77.9 18.1 %collective-permute-start.24 = (bf16[4,4,176,256]{3,2,1,0:T(8,128)(2,1)}, bf16[4,4,176,256]{3,2,1,0:T(8,128)(2,1)S(1)}, u32[]{:S(2)}, u32[]{:S(2)}) collective-permute-start(bf16[4,4,176,256]{3,2,1,0:T(8,128)(2,1)} %collective-permute-done.16.rest_2_), channel_id=1, source_target_pairs={{0,1},{1,0},{2,3},{3,2},{4,5},{5,4},{6,7},{7,6},{8,9},{9,8},{10,11... | collective-permute-start | bytes 4325384 | tf_op jit(solution)/shard_map/ppermute | solution.py:42
  78.0 20.5 %collective-permute-start.22 = (bf16[4,4,176,256]{3,2,1,0:T(8,128)(2,1)}, bf16[4,4,176,256]{3,2,1,0:T(8,128)(2,1)S(1)}, u32[]{:S(2)}, u32[]{:S(2)}) collective-permute-start(bf16[4,4,176,256]{3,2,1,0:T(8,128)(2,1)} %collective-permute-done.16.rest_2_), channel_id=1, source_target_pairs={{0,2},{1,7},{2,4},{3,1},{4,6},{5,3},{6,0},{7,5},{8,10},{9,15},{10,... | collective-permute-start | bytes 4325384 | tf_op jit(solution)/shard_map/ppermute | solution.py:38
  98.5 20.2 %collective-permute-start.25 = (bf16[4,4,176,256]{3,2,1,0:T(8,128)(2,1)S(1)}, bf16[4,4,176,256]{3,2,1,0:T(8,128)(2,1)S(1)}, u32[]{:S(2)}, u32[]{:S(2)}) collective-permute-start(bf16[4,4,176,256]{3,2,1,0:T(8,128)(2,1)S(1)} %collective-permute-done.19.rest_0_), channel_id=1, source_target_pairs={{0,64},{1,97},{2,66},{3,99},{4,68},{5,101},{6,70},{7,103},{8,72},{... | collective-permute-start | bytes 4325384 | tf_op jit(solution)/shard_map/ppermute | solution.py:38
  99.4 20.2 %collective-permute-start.26 = (bf16[4,4,176,256]{3,2,1,0:T(8,128)(2,1)S(1)}, bf16[4,4,176,256]{3,2,1,0:T(8,128)(2,1)S(1)}, u32[]{:S(2)}, u32[]{:S(2)}) collective-permute-start(bf16[4,4,176,256]{3,2,1,0:T(8,128)(2,1)S(1)} %collective-permute-done.20.rest_1_), channel_id=1, source_target_pairs={{0,8},{1,25},{2,10},{3,27},{4,12},{5,29},{6,14},{7,31},{8,16},{9,1... | collective-permute-start | bytes 4325384 | tf_op jit(solution)/shard_map/ppermute | solution.py:38
  99.4 20.2 %collective-permute-start.29 = (bf16[4,4,176,256]{3,2,1,0:T(8,128)(2,1)S(1)}, bf16[4,4,176,256]{3,2,1,0:T(8,128)(2,1)}, u32[]{:S(2)}, u32[]{:S(2)}) collective-permute-start(bf16[4,4,176,256]{3,2,1,0:T(8,128)(2,1)S(1)} %collective-permute-done.20.rest_1_), channel_id=1, source_target_pairs={{0,1},{1,0},{2,3},{3,2},{4,5},{5,4},{6,7},{7,6},{8,9},{9,8},{10,11... | collective-permute-start | bytes 4325384 | tf_op jit(solution)/shard_map/ppermute | solution.py:42
  102.1 17.5 %collective-permute-start.30 = (bf16[4,4,176,256]{3,2,1,0:T(8,128)(2,1)S(1)}, bf16[4,4,176,256]{3,2,1,0:T(8,128)(2,1)}, u32[]{:S(2)}, u32[]{:S(2)}) collective-permute-start(bf16[4,4,176,256]{3,2,1,0:T(8,128)(2,1)S(1)} %collective-permute-done.22.rest_2_), channel_id=1, source_target_pairs={{0,1},{1,0},{2,3},{3,2},{4,5},{5,4},{6,7},{7,6},{8,9},{9,8},{10,11... | collective-permute-start | bytes 4325384 | tf_op jit(solution)/shard_map/ppermute | solution.py:42
  102.1 20.4 %collective-permute-start.28 = (bf16[4,4,176,256]{3,2,1,0:T(8,128)(2,1)S(1)}, bf16[4,4,176,256]{3,2,1,0:T(8,128)(2,1)}, u32[]{:S(2)}, u32[]{:S(2)}) collective-permute-start(bf16[4,4,176,256]{3,2,1,0:T(8,128)(2,1)S(1)} %collective-permute-done.22.rest_2_), channel_id=1, source_target_pairs={{0,2},{1,7},{2,4},{3,1},{4,6},{5,3},{6,0},{7,5},{8,10},{9,15},{10,... | collective-permute-start | bytes 4325384 | tf_op jit(solution)/shard_map/ppermute | solution.py:38
  122.5 12.5 collective-permute-start.31
  122.5 12.5 collective-permute-start.32
  123.0 12.0 collective-permute-start.33
  349.8 18.6 %collective-permute-start = (bf16[2,128,512]{2,1,0:T(8,128)(2,1)S(1)}, bf16[2,128,512]{2,1,0:T(8,128)(2,1)S(1)}, u32[]{:S(2)}, u32[]{:S(2)}) collective-permute-start(bf16[2,128,512]{2,1,0:T(8,128)(2,1)S(1)} %copy.147), channel_id=1, source_target_pairs={{0,1},{1,2},{2,3},{3,4},{4,5},{5,6},{6,7},{7,8},{8,9},{9,10},{10,1... | collective-permute-start | bytes 786440 | tf_op jit(solution)/shard_map/cond/branch_0_fun/while/body/eval_jaxpr/ppermute | solution.py:536
  368.4 11.6 collective-permute-start
  380.0 11.6 collective-permute-start
  (108 other events, 1018.8 us)

commit v3 on v2

--- a/solution.py
+++ b/solution.py
@@ -274,6 +274,13 @@
     def main_tile(r, i, own):
         return gathered(r, groups_of(r, i, own), 0, TOK, 0, TOK)
 
+    def whole_tile(r):
+        if r == 0:
+            groups = [(near, j) for j in range(4)]
+        else:
+            groups = [(side, led(side, j, True)) for j in range(2) for side in sides]
+        return gathered(r, groups, 0, TOK, 0, TOK)
+
     def third_tile(r, i, own):
         if r == 0:
             side = near if own is True else active
@@ -413,7 +420,7 @@
             for i in range(2):
                 acc_loads[r, i].wait()
         if r != 0 or prompt_usable:
-            loop(tiles(r), lambda i, r=r: prompt_tile(r, *main_tile(r, i, True)))
+            prompt_tile(r, *whole_tile(r))
         settle(r, 0)
     if first:
         own_block(3)

time: 1380 us -> 1390 us (level)
  transfers between devices with their start and end apart: 97 -> 97, of which waited for: 83 -> 83; matrix products, arithmetic and copies ran while one was open for 4% -> 4% of each run, Pallas kernels for 3% -> 4%
where the time goes in v3:
time: 1390 us; the launch traced here: 1370 us
  waiting for transfers between devices  725 us (52%)
  matrix products  269 us (19%)
  local copies, waits for them, and re-layouts  160 us (12%)
  other arithmetic  107 us (8%)
  Pallas kernels  61.9 us (4%)
  starting transfers between devices  38.3 us (3%)
    ppermute x64, waiting for transfers between devices, collect(): return (lax.ppermute(shard, 'blk', right), cache)  679 us
    dot_general x48, matrix products, turn(): jnp.einsum('tkgd,skd->kgts', query, part_k, preferred_element_type=jnp.fl...  143 us
    dot_general x48, matrix products, turn(): jnp.einsum('kgts,skd->kgtd', w.astype(jnp.bfloat16), part_v, preferred_el...  126 us
    reduce_sum x48, other arithmetic, turn(): total = total * shrink + jnp.sum(w, axis=-1)  95.8 us
    pallas_call x5, Pallas kernels, run_stage(): pl.pallas_call(functools.partial(stage_kernel, t), out_shape=outs, in_spe...  59.6 us
    dynamic_update_slice x128, local copies, waits for them, and re-layouts, collect(): lax.dynamic_update_slice(cache, shard, (0, (place - i) % count * tok, 0))  59.3 us
    ppermute x21, waiting for transfers between devices, moved(): return lax.ppermute(value, AX, route)  44.7 us
    another operation x70, local copies, waits for them, and re-layouts  29 us
  transfers between devices with their start and end apart: 97, of which 83 were waited for; matrix products, arithmetic and copies ran while one was open for 4% of the time, Pallas kernels for 4%

profile of v3, /device:TPU:0, one launch (start us, length us, event | category | flops | bytes accessed | tf_op | source)
XLA Modules:
  0.0 1371.0 jit_solution(328753956793242915)
XLA Ops:
  78.5 13.2 stage1.1
  103.0 15.6 %stage2.1 = (f32[4,128,1024]{2,1,0:T(8,128)}, f32[4,8,1024]{2,1,0:T(8,128)S(1)}, f32[4,512,128]{2,1,0:T(8,128)S(1)}, f32[4,512,128]{2,1,0:T(8,128)S(1)}, bf16[2,...) custom-call(s32[8]{0:T(128)S(1)} %stack.27.meta, ...), custom_call_target="tpu_custom_call", output_to_operand_aliasing={{0}: (10, {}), {1}: (11, {}), {2}: (12, {}), {3}: (13, {}),... | custom-call | flops 12884901888 | bytes 31457280 | tf_op jit(solution)/shard_map/stage2/pallas_call | solution.py:504
  123.1 12.2 stage3.1
  148.8 1222.0 %conditional.1 = (bf16[2,32,4096]{2,1,0:T(8,128)(2,1)}, bf16[1,128,4096]{2,1,0:T(8,128)(2,1)}) conditional(s32[]{:T(128)} %convert_element_type.76, (bf16[2,32,512]{2,1,0:T(8,128)(2,1)S(1)}, bf16[2,32,4096]{2,1,0:T(8,128)(2,1)S(1)}, bf16[2,32,512]{2,1,0:T(8,128)(2,1)S(1)}, bf16[2,8192,512]{2,1,0:T(8,128)(2,1)}, s32[32]{0:T(128)S(1)}, ...), branch_computations={%region_2.19_spmd, %region_19.20_spmd} | conditional | flops 1657168640 | bytes 260901488 | solution.py:650
  150.2 21.2 %copy.82 = bf16[2,8192,512]{1,2,0:T(8,128)(2,1)} copy(bf16[2,8192,512]{2,1,0:T(8,128)(2,1)} %get-tuple-element.876) | data formatting | bytes 33554432 | tf_op jit(solution)/shard_map
  171.4 11.6 fusion.78
  183.0 12.0 copy.62
  195.0 11.9 copy.64
  207.0 68.5 %while.66 = (s32[]{:T(128)}, f32[4,8,32]{2,1,0:T(8,128)S(1)}, f32[4,8,32]{2,1,0:T(8,128)S(1)}, f32[4,8,32,128]{3,2,1,0:T(8,128)S(1)}, s32[32]{0:T(128)S(1)}, /*i...) while((s32[]{:T(128)}, f32[4,8,32]{2,1,0:T(8,128)S(1)}, ...), condition=%wide.region_12.12_spmd, body=%wide.region_9.11_spmd.sunk | while | flops 275532288 | bytes 8786223 | solution.py:572
  276.9 68.5 %while.65 = (s32[]{:T(128)}, f32[4,8,32]{2,1,0:T(8,128)S(1)}, f32[4,8,32]{2,1,0:T(8,128)S(1)}, f32[4,8,32,128]{3,2,1,0:T(8,128)S(1)}, s32[32]{0:T(128)S(1)}, /*i...) while((s32[]{:T(128)}, f32[4,8,32]{2,1,0:T(8,128)S(1)}, ...), condition=%wide.region_6.6_spmd, body=%wide.region_3.5_spmd.sunk | while | flops 275532288 | bytes 8786223 | solution.py:572
  352.8 747.9 %while.67 = (s32[]{:T(128)}, bf16[2,128,512]{2,1,0:T(8,128)(2,1)S(1)}, bf16[2,8192,512]{1,2,0:T(8,128)(2,1)}, s32[]{:T(128)}, s32[]{:T(128)}, /*index=5*/s32[]{:T(128)}, s32[]{:T(128)}, s32[]{:T(128)}, s32[]{:T(128)}, s32[]{:T(128)}) while((s32[]{:T(128)}, bf16[2,128,512]{2,1,0:T(8,128)(2,1)S(1)}, bf16[2,8192,512]{1,2,0:T(8,128)(2,1)}, ...), condition=%wide.region_14.14_spmd, body=%wide.region_13.13_spmd.sunk | while | flops 18 | bytes 2621752 | solution.py:547
  354.3 14.8 %collective-permute-done = bf16[2,128,512]{2,1,0:T(8,128)(2,1)S(1)} collective-permute-done((bf16[2,128,512]{2,1,0:T(8,128)(2,1)S(1)}, bf16[2,128,512]{2,1,0:T(8,128)(2,1)S(1)}, u32[]{:S(2)}, u32[]{:S(2)}) %collective-permute-start) | collective-permute-done | bytes 262176 | tf_op jit(solution)/shard_map/cond/branch_0_fun/while/body/eval_jaxpr/ppermute | solution.py:543
  648.8 10.6 collective-permute-done
  672.1 10.6 collective-permute-done
  683.7 10.6 collective-permute-done
  718.5 10.6 collective-permute-done
  730.1 10.6 collective-permute-done
  741.7 10.6 collective-permute-done
  823.0 10.6 collective-permute-done
  950.7 10.6 collective-permute-done
  985.6 10.6 collective-permute-done
  1020.4 10.6 collective-permute-done
  1100.6 11.6 fusion.77
  1113.6 254.5 %while.68 = (s32[]{:T(128)}, f32[4,8,128]{2,1,0:T(8,128)S(1)}, f32[4,8,128]{2,1,0:T(8,128)S(1)}, f32[4,8,128,128]{3,2,1,0:T(8,128)S(1)}, bf16[8192,4,128]{0,2,1:...) while((s32[]{:T(128)}, f32[4,8,128]{2,1,0:T(8,128)S(1)}, ...), condition=%wide.region_18.18_spmd.clone, body=%wide.region_15.17_spmd.clone.sunk | while | flops 1102664448 | bytes 65541336 | solution.py:572
  (906 shorter events, 1131.3 us)
Async XLA Ops:
  31.2 12.6 collective-permute-start.10
  31.8 12.5 collective-permute-start.11
  35.1 12.5 collective-permute-start.12
  49.2 20.4 %collective-permute-start.13 = (bf16[4,4,176,256]{3,2,1,0:T(8,128)(2,1)S(1)}, bf16[4,4,176,256]{3,2,1,0:T(8,128)(2,1)}, u32[]{:S(2)}, u32[]{:S(2)}) collective-permute-start(bf16[4,4,176,256]{3,2,1,0:T(8,128)(2,1)S(1)} %pad_maximum_fusion.2.rest_0_), channel_id=1, source_target_pairs={{0,64},{1,97},{2,66},{3,99},{4,68},{5,101},{6,70},{7,103},{8,72},{... | collective-permute-start | bytes 4325384 | tf_op jit(solution)/shard_map/ppermute | solution.py:38
  50.7 20.3 %collective-permute-start.14 = (bf16[4,4,176,256]{3,2,1,0:T(8,128)(2,1)S(1)}, bf16[4,4,176,256]{3,2,1,0:T(8,128)(2,1)}, u32[]{:S(2)}, u32[]{:S(2)}) collective-permute-start(bf16[4,4,176,256]{3,2,1,0:T(8,128)(2,1)S(1)} %pad_maximum_fusion.3.rest_1_), channel_id=1, source_target_pairs={{0,8},{1,25},{2,10},{3,27},{4,12},{5,29},{6,14},{7,31},{8,16},{9,1... | collective-permute-start | bytes 4325384 | tf_op jit(solution)/shard_map/ppermute | solution.py:38
  50.7 20.3 %collective-permute-start.17 = (bf16[4,4,176,256]{3,2,1,0:T(8,128)(2,1)S(1)}, bf16[4,4,176,256]{3,2,1,0:T(8,128)(2,1)}, u32[]{:S(2)}, u32[]{:S(2)}) collective-permute-start(bf16[4,4,176,256]{3,2,1,0:T(8,128)(2,1)S(1)} %pad_maximum_fusion.3.rest_1_), channel_id=1, source_target_pairs={{0,1},{1,0},{2,3},{3,2},{4,5},{5,4},{6,7},{7,6},{8,9},{9,8},{10,11... | collective-permute-start | bytes 4325384 | tf_op jit(solution)/shard_map/ppermute | solution.py:42
  50.7 20.3 %collective-permute-start.18 = (bf16[4,4,176,256]{3,2,1,0:T(8,128)(2,1)}, bf16[4,4,176,256]{3,2,1,0:T(8,128)(2,1)}, u32[]{:S(2)}, u32[]{:S(2)}) collective-permute-start(bf16[4,4,176,256]{3,2,1,0:T(8,128)(2,1)} %pad_maximum_fusion.4.rest_2_), channel_id=1, source_target_pairs={{0,1},{1,0},{2,3},{3,2},{4,5},{5,4},{6,7},{7,6},{8,9},{9,8},{10,11... | collective-permute-start | bytes 4325384 | tf_op jit(solution)/shard_map/ppermute | solution.py:42
  53.6 20.5 %collective-permute-start.16 = (bf16[4,4,176,256]{3,2,1,0:T(8,128)(2,1)}, bf16[4,4,176,256]{3,2,1,0:T(8,128)(2,1)}, u32[]{:S(2)}, u32[]{:S(2)}) collective-permute-start(bf16[4,4,176,256]{3,2,1,0:T(8,128)(2,1)} %pad_maximum_fusion.4.rest_2_), channel_id=1, source_target_pairs={{0,2},{1,7},{2,4},{3,1},{4,6},{5,3},{6,0},{7,5},{8,10},{9,15},{10,... | collective-permute-start | bytes 4325384 | tf_op jit(solution)/shard_map/ppermute | solution.py:38
  74.1 20.4 %collective-permute-start.19 = (bf16[4,4,176,256]{3,2,1,0:T(8,128)(2,1)}, bf16[4,4,176,256]{3,2,1,0:T(8,128)(2,1)S(1)}, u32[]{:S(2)}, u32[]{:S(2)}) collective-permute-start(bf16[4,4,176,256]{3,2,1,0:T(8,128)(2,1)} %collective-permute-done.13.rest_0_), channel_id=1, source_target_pairs={{0,64},{1,97},{2,66},{3,99},{4,68},{5,101},{6,70},{7,103},{8,72},{... | collective-permute-start | bytes 4325384 | tf_op jit(solution)/shard_map/ppermute | solution.py:38
  75.6 20.4 %collective-permute-start.20 = (bf16[4,4,176,256]{3,2,1,0:T(8,128)(2,1)}, bf16[4,4,176,256]{3,2,1,0:T(8,128)(2,1)S(1)}, u32[]{:S(2)}, u32[]{:S(2)}) collective-permute-start(bf16[4,4,176,256]{3,2,1,0:T(8,128)(2,1)} %collective-permute-done.14.rest_1_), channel_id=1, source_target_pairs={{0,8},{1,25},{2,10},{3,27},{4,12},{5,29},{6,14},{7,31},{8,16},{9,1... | collective-permute-start | bytes 4325384 | tf_op jit(solution)/shard_map/ppermute | solution.py:38
  75.6 20.4 %collective-permute-start.23 = (bf16[4,4,176,256]{3,2,1,0:T(8,128)(2,1)}, bf16[4,4,176,256]{3,2,1,0:T(8,128)(2,1)S(1)}, u32[]{:S(2)}, u32[]{:S(2)}) collective-permute-start(bf16[4,4,176,256]{3,2,1,0:T(8,128)(2,1)} %collective-permute-done.14.rest_1_), channel_id=1, source_target_pairs={{0,1},{1,0},{2,3},{3,2},{4,5},{5,4},{6,7},{7,6},{8,9},{9,8},{10,11... | collective-permute-start | bytes 4325384 | tf_op jit(solution)/shard_map/ppermute | solution.py:42
  77.9 18.1 %collective-permute-start.24 = (bf16[4,4,176,256]{3,2,1,0:T(8,128)(2,1)}, bf16[4,4,176,256]{3,2,1,0:T(8,128)(2,1)S(1)}, u32[]{:S(2)}, u32[]{:S(2)}) collective-permute-start(bf16[4,4,176,256]{3,2,1,0:T(8,128)(2,1)} %collective-permute-done.16.rest_2_), channel_id=1, source_target_pairs={{0,1},{1,0},{2,3},{3,2},{4,5},{5,4},{6,7},{7,6},{8,9},{9,8},{10,11... | collective-permute-start | bytes 4325384 | tf_op jit(solution)/shard_map/ppermute | solution.py:42
  77.9 20.5 %collective-permute-start.22 = (bf16[4,4,176,256]{3,2,1,0:T(8,128)(2,1)}, bf16[4,4,176,256]{3,2,1,0:T(8,128)(2,1)S(1)}, u32[]{:S(2)}, u32[]{:S(2)}) collective-permute-start(bf16[4,4,176,256]{3,2,1,0:T(8,128)(2,1)} %collective-permute-done.16.rest_2_), channel_id=1, source_target_pairs={{0,2},{1,7},{2,4},{3,1},{4,6},{5,3},{6,0},{7,5},{8,10},{9,15},{10,... | collective-permute-start | bytes 4325384 | tf_op jit(solution)/shard_map/ppermute | solution.py:38
  98.5 20.2 %collective-permute-start.25 = (bf16[4,4,176,256]{3,2,1,0:T(8,128)(2,1)S(1)}, bf16[4,4,176,256]{3,2,1,0:T(8,128)(2,1)S(1)}, u32[]{:S(2)}, u32[]{:S(2)}) collective-permute-start(bf16[4,4,176,256]{3,2,1,0:T(8,128)(2,1)S(1)} %collective-permute-done.19.rest_0_), channel_id=1, source_target_pairs={{0,64},{1,97},{2,66},{3,99},{4,68},{5,101},{6,70},{7,103},{8,72},{... | collective-permute-start | bytes 4325384 | tf_op jit(solution)/shard_map/ppermute | solution.py:38
  99.5 20.2 %collective-permute-start.26 = (bf16[4,4,176,256]{3,2,1,0:T(8,128)(2,1)S(1)}, bf16[4,4,176,256]{3,2,1,0:T(8,128)(2,1)S(1)}, u32[]{:S(2)}, u32[]{:S(2)}) collective-permute-start(bf16[4,4,176,256]{3,2,1,0:T(8,128)(2,1)S(1)} %collective-permute-done.20.rest_1_), channel_id=1, source_target_pairs={{0,8},{1,25},{2,10},{3,27},{4,12},{5,29},{6,14},{7,31},{8,16},{9,1... | collective-permute-start | bytes 4325384 | tf_op jit(solution)/shard_map/ppermute | solution.py:38
  99.5 20.2 %collective-permute-start.29 = (bf16[4,4,176,256]{3,2,1,0:T(8,128)(2,1)S(1)}, bf16[4,4,176,256]{3,2,1,0:T(8,128)(2,1)}, u32[]{:S(2)}, u32[]{:S(2)}) collective-permute-start(bf16[4,4,176,256]{3,2,1,0:T(8,128)(2,1)S(1)} %collective-permute-done.20.rest_1_), channel_id=1, source_target_pairs={{0,1},{1,0},{2,3},{3,2},{4,5},{5,4},{6,7},{7,6},{8,9},{9,8},{10,11... | collective-permute-start | bytes 4325384 | tf_op jit(solution)/shard_map/ppermute | solution.py:42
  101.8 18.0 %collective-permute-start.30 = (bf16[4,4,176,256]{3,2,1,0:T(8,128)(2,1)S(1)}, bf16[4,4,176,256]{3,2,1,0:T(8,128)(2,1)}, u32[]{:S(2)}, u32[]{:S(2)}) collective-permute-start(bf16[4,4,176,256]{3,2,1,0:T(8,128)(2,1)S(1)} %collective-permute-done.22.rest_2_), channel_id=1, source_target_pairs={{0,1},{1,0},{2,3},{3,2},{4,5},{5,4},{6,7},{7,6},{8,9},{9,8},{10,11... | collective-permute-start | bytes 4325384 | tf_op jit(solution)/shard_map/ppermute | solution.py:42
  101.8 20.8 %collective-permute-start.28 = (bf16[4,4,176,256]{3,2,1,0:T(8,128)(2,1)S(1)}, bf16[4,4,176,256]{3,2,1,0:T(8,128)(2,1)}, u32[]{:S(2)}, u32[]{:S(2)}) collective-permute-start(bf16[4,4,176,256]{3,2,1,0:T(8,128)(2,1)S(1)} %collective-permute-done.22.rest_2_), channel_id=1, source_target_pairs={{0,2},{1,7},{2,4},{3,1},{4,6},{5,3},{6,0},{7,5},{8,10},{9,15},{10,... | collective-permute-start | bytes 4325384 | tf_op jit(solution)/shard_map/ppermute | solution.py:38
  122.6 12.8 collective-permute-start.31
  122.6 12.8 collective-permute-start.32
  123.1 12.3 collective-permute-start.33
  352.8 16.3 %collective-permute-start = (bf16[2,128,512]{2,1,0:T(8,128)(2,1)S(1)}, bf16[2,128,512]{2,1,0:T(8,128)(2,1)S(1)}, u32[]{:S(2)}, u32[]{:S(2)}) collective-permute-start(bf16[2,128,512]{2,1,0:T(8,128)(2,1)S(1)} %copy.147), channel_id=1, source_target_pairs={{0,1},{1,2},{2,3},{3,4},{4,5},{5,6},{6,7},{7,8},{8,9},{9,10},{10,1... | collective-permute-start | bytes 786440 | tf_op jit(solution)/shard_map/cond/branch_0_fun/while/body/eval_jaxpr/ppermute | solution.py:543
  369.1 11.6 collective-permute-start
  380.7 11.6 collective-permute-start
  (108 other events, 1035.0 us)
